TPU v7x, 32 devices: a whole 2x2x4 slice. The times are simulated.
32 devices in a mesh: lang: 4 (over x, core), seq: 8 (over z, y).
Axes of the slice: x: 2, y: 2, z: 4, core: 2. Of those that a mesh axis runs over, the one named last changes fastest.
Arguments:
- prompt_rows: bfloat16 [4096, 2048], P(('lang', 'seq')), may hold values from -6 to 6
- expert_ids: int32 [4096, 2], P(('lang', 'seq')), may hold values from 0 to 3, all different within a row; in each aligned block of 128 rows (0 to 127, 128 to 255, ...) at most 96 rows name the same one
- expert_gates: float32 [4096, 2], P(('lang', 'seq')), may hold values from 0.25 to 1
- w_gate: bfloat16 [4, 2048, 704], P('lang', 'seq'), may hold values from -0.125 to 0.125
- w_up: bfloat16 [4, 2048, 704], P('lang', 'seq'), may hold values from -0.125 to 0.125
- w_down: bfloat16 [4, 704, 2048], P('lang', None, 'seq'), may hold values from -0.21875 to 0.21875
- w_kv: bfloat16 [2048, 2, 1024], P(None, None, 'seq'), may hold values from -0.125 to 0.125
- prompt_lengths: int32 [8], P('lang'), may hold values from 128 to 512, as said below
- latent_q: bfloat16 [8, 512, 1024], P('lang', 'seq'), may hold values from -5 to 5
- latent_k: bfloat16 [8, 512, 1024], P('lang', 'seq'), may hold values from -5 to 5
- latent_v: bfloat16 [8, 512, 1024], P('lang', 'seq'), may hold values from -6 to 6
- grad_out: bfloat16 [8, 512, 1024], P('lang', 'seq'), may hold values from -6 to 6
Outputs:
- attended: bfloat16 [8, 512, 1024], P('lang', 'seq')
- grad_latent: bfloat16 [3, 8, 512, 1024], P(None, 'lang', 'seq')
- grad_wkv: float32 [2048, 2, 1024], P(None, None, 'seq')
Inputs may be any that keep to these rules, and one draw needn't show every extreme that they name: `expert_ids`: in each aligned block of 128 rows (the rows of one device) no expert is named by more than 96 rows. `prompt_lengths`: the first of each group of 2 pages uses its whole prompt.
All inputs are finite; a program needn't handle non-finite values.
Results may differ from a plain program's by a relative error of at most 0.03.
Values may be sent and summed in bfloat16 or wider, within the bound.
No kernel may reach another device: no remote copies, remote signals or barrier semaphores. Data moves between devices by JAX's collectives and lax.ppermute only.
A program may use at most 128 MiB of HBM per device.

v0:
```python
import functools
import math

import jax
import jax.numpy as jnp
from jax import lax
from jax.experimental import pallas as pl
from jax.experimental.pallas import tpu as pltpu
from jax.sharding import PartitionSpec as P

HD = 128
PAIR = 2
TILE = 16
STEP = 4
NT = (((1,), (1,)), ((), ()))
TN = (((0,), (0,)), ((), ()))
F32 = jnp.float32
BF16 = jnp.bfloat16


def params():
    return pltpu.CompilerParams(vmem_limit_bytes=60 * 2**20)


def vmem():
    return pl.BlockSpec(memory_space=pltpu.VMEM)


def smem():
    return pl.BlockSpec(memory_space=pltpu.SMEM)


def dot(a, b):
    return jnp.dot(a, b, preferred_element_type=F32)


def ring_order(count):
    return list(range(0, count, 2)) + list(range(count - 1, 0, -2))


def ring_pairs(count, step):
    order = ring_order(count)
    return [(order[i], order[(i + step) % count]) for i in range(count)]


def ring_places(count):
    order = ring_order(count)
    return jnp.array([[order.index(i) for i in range(count)], order], jnp.int32)


def ring_gather(block, count):
    ahead = ring_pairs(count, 1)
    back = ring_pairs(count, -1)
    half_rows = block.shape[0] // 2
    parts = [(0, [block])]
    up, down = block, block
    for distance in range(1, count // 2):
        up = lax.ppermute(up, "seq", ahead)
        down = lax.ppermute(down, "seq", back)
        parts.append((-distance, [up]))
        parts.append((distance, [down]))
    last_up = lax.ppermute(up[:half_rows], "seq", ahead)
    last_down = lax.ppermute(down[half_rows:], "seq", back)
    parts.append((count // 2, [last_up, last_down]))
    return parts


def whole(refs):
    if len(refs) == 1:
        return refs[0][...]
    return jnp.concatenate([ref[...] for ref in refs], axis=0)


def xor_swap(array, axis, mask):
    count = lax.axis_size(axis)
    return lax.ppermute(array, axis, [(i, i ^ mask) for i in range(count)])


def gather_lang(rows, far):
    langs = lax.axis_size("lang")
    mask = langs // 2
    blocks = {0: rows, mask: far}
    while mask > 1:
        mask //= 2
        for lang, block in list(blocks.items()):
            blocks[lang | mask] = xor_swap(block, "lang", mask)
    return [blocks[lang] for lang in range(langs)]


def reduce_rows(keep, send, pair_first, after):
    langs = lax.axis_size("lang")

    def over_pair(parts):
        kept, sent = parts
        arrived = xor_swap(tie(sent.astype(BF16), after), "seq", PAIR)
        return kept + arrived.astype(F32)

    arrived = xor_swap(send, "lang", 1)
    halves = [keep[side].astype(F32) + arrived[side].astype(F32) for side in range(2)]
    if pair_first:
        halves = [over_pair(halves)]
    mask = 2
    while mask < langs:
        sent = jnp.stack([half[1::2] for half in halves]).astype(BF16)
        arrived = xor_swap(sent, "lang", mask).astype(F32)
        halves = [half[0::2] + arrived[side] for side, half in enumerate(halves)]
        mask *= 2
    total = halves[0] if pair_first else over_pair(halves)
    return total[0].astype(BF16)


def split_halves(block, seq_index):
    rows = block.shape[0] // 2
    side = (seq_index // PAIR) % 2
    mine = lax.dynamic_slice_in_dim(block, side * rows, rows, 0)
    other = lax.dynamic_slice_in_dim(block, (1 - side) * rows, rows, 0)
    return mine, other


def tie(array, *others):
    return lax.optimization_barrier((array, *others))[0]


def gather_inputs(gate, up, down, rows, seq_index, count, aside, own_sums):
    top = lax.axis_size("lang") // 2
    mine, other = zip(*[split_halves(block, seq_index) for block in (gate, up, down)])
    mine = jnp.concatenate(mine, axis=0)
    other = jnp.concatenate(other, axis=0)
    along, across = {0: mine}, {}
    along[2 * PAIR] = xor_swap(mine, "seq", 2 * PAIR)
    along[PAIR] = xor_swap(other, "seq", PAIR)
    across[1] = xor_swap(mine, "seq", 1)
    ready = [2 * PAIR, PAIR]
    pair_rows = far = rows
    for mask in range(3 * PAIR, count, PAIR):
        held = other if mask & PAIR else mine
        arrived = [along[done] for done in ready]
        held, pair_rows, far, across[1], aside, arrived = lax.optimization_barrier(
            (held, pair_rows, far, across[1], aside, arrived)
        )
        along[mask] = xor_swap(held, "seq", mask)
        for done, array in zip(ready, arrived):
            along[done] = array
            across[done | 1] = xor_swap(array, "seq", 1)
        if mask == 3 * PAIR:
            pair_rows = xor_swap(pair_rows, "seq", PAIR)
            far = xor_swap(far, "lang", top)
        ready = [mask]
    last = ready[0]
    early = [across[mask | 1] for mask in along if mask not in (0, last)]
    pair_rows, far, along[last], early = lax.optimization_barrier(
        (pair_rows, far, along[last], early)
    )
    for mask, array in zip([mask for mask in along if mask not in (0, last)], early):
        across[mask | 1] = array
    own_blocks = gather_lang(rows, far)
    first = sorted((along | across).items())
    first = [item for item in first if item[0] != last]
    sums = own_sums(own_blocks, first)
    across[last | 1], pair_far, sums = lax.optimization_barrier(
        (xor_swap(along[last], "seq", 1), xor_swap(pair_rows, "lang", top), sums)
    )
    pair_blocks = gather_lang(pair_rows, pair_far)
    late = [(mask, shard) for mask, shard in ((last, along[last]), (last | 1, across[last | 1]))]
    return along, across, own_blocks, pair_blocks, first, late, sums, aside


def pack_body(*refs):
    out = refs[-1]
    for which, ref in enumerate(refs[:-1]):
        for head in range(out.shape[0]):
            out[head, which] = ref[:, :, head * HD : (head + 1) * HD]


def pack(arrays):
    pages, rows, width = arrays[0].shape
    shape = (width // HD, len(arrays), pages, rows, HD)
    return pl.pallas_call(
        pack_body,
        out_shape=jax.ShapeDtypeStruct(shape, BF16),
        in_specs=[vmem()] * len(arrays),
        out_specs=vmem(),
        compiler_params=params(),
        name="pack",
    )(*arrays)


def unpack_body(packed, attended, grads):
    for head in range(packed.shape[0]):
        cols = slice(head * HD, (head + 1) * HD)
        attended[:, :, cols] = packed[head, 0]
        for which in range(3):
            grads[which, :, :, cols] = packed[head, which + 1]


def unpack(packed):
    heads, _, pages, rows, _ = packed.shape
    return pl.pallas_call(
        unpack_body,
        out_shape=(
            jax.ShapeDtypeStruct((pages, rows, heads * HD), BF16),
            jax.ShapeDtypeStruct((3, pages, rows, heads * HD), BF16),
        ),
        in_specs=[vmem()],
        out_specs=(vmem(), vmem()),
        compiler_params=params(),
        name="unpack",
    )(packed)


def with_gates(rows, expert_ids, expert_gates):
    picks = expert_ids.shape[1]
    fields = [expert_ids.T.astype(F32)]
    rest = expert_gates.T
    for _ in range(3):
        term = lax.reduce_precision(rest, 8, 7)
        fields.append(term)
        rest = rest - term
    tile = jnp.concatenate(fields, axis=0).astype(BF16)
    tile = jnp.pad(tile, ((0, TILE - 4 * picks), (0, rows.shape[1] - rows.shape[0])))
    return jnp.concatenate([rows, tile], axis=0)


def shard_sums(tokens, rows, seq, masks, shards):
    chunk = shards.shape[1] // len(masks)
    starts = [pl.multiple_of((seq ^ mask) * chunk, chunk) for mask in masks]
    inputs = [
        jnp.concatenate([ref[:rows, pl.ds(start, chunk)] for start in starts], axis=1)
        for ref in tokens
    ]
    inputs = jnp.concatenate(inputs, axis=0)
    return lax.dot_general(inputs, shards, NT, preferred_element_type=F32)


def beside(weights):
    both = 2 * (weights[0].shape[0] // 3)
    return jnp.concatenate([weight[:both, :] for weight in weights], axis=1)


def hidden_sums_stage(place, row_blocks, parts):
    blocks = len(row_blocks)
    rows = row_blocks[0].shape[0] - TILE
    masks = [mask for mask, _ in parts]

    def body(*refs):
        tokens, weights, out = refs[1 : 1 + blocks], refs[1 + blocks : -1], refs[-1]
        shards = beside(weights)
        for at in range(0, blocks, STEP):
            here = slice(at * rows, (at + STEP) * rows)
            out[here] = shard_sums(tokens[at : at + STEP], rows, refs[0][1], masks, shards)

    operands = [place, *row_blocks, *[array for _, array in parts]]
    shape = (rows * blocks, 2 * (parts[0][1].shape[0] // 3))
    return pl.pallas_call(
        body,
        out_shape=jax.ShapeDtypeStruct(shape, F32),
        in_specs=[smem()] + [vmem()] * (len(operands) - 1),
        out_specs=vmem(),
        compiler_params=params(),
        name="hidden_sums",
    )(*operands)


def expert_stage(place, own_blocks, pair_blocks, first, late, sums, picks):
    blocks = len(own_blocks)
    rows = own_blocks[0].shape[0] - TILE
    half = rows * blocks
    inner = sums.shape[1] // 2
    chunk = first[0][1].shape[1]
    parts = first + late
    width = chunk * len(parts) // 2

    def body(*refs):
        lang, seq = refs[0][0], refs[0][1]
        tokens = refs[1 : 1 + 2 * blocks]
        weights = refs[1 + 2 * blocks : -6]
        old, hidden = refs[-6], refs[-1]
        outs = refs[-5:-1]
        masks = [mask for mask, _ in parts]
        late_shards = beside(weights[len(first) :])
        shards = beside(weights)
        for at in range(0, 2 * blocks, STEP):
            group = tokens[at : at + STEP]
            if at < blocks:
                total = shard_sums(group, rows, seq, masks[len(first) :], late_shards)
                total = total + old[at * rows : (at + STEP) * rows]
            else:
                total = shard_sums(group, rows, seq, masks, shards)
            for block, ref in enumerate(group):
                fields = ref[rows:, :rows].astype(F32)
                weight = jnp.zeros((1, rows), F32)
                for pick in range(picks):
                    terms = [fields[row : row + 1] for row in range(pick, 4 * picks, picks)]
                    named = terms[0] == lang.astype(F32)
                    weight = weight + jnp.where(named, terms[1] + terms[2] + terms[3], 0.0)
                weight = jnp.broadcast_to(weight, (rows, rows)).T[:, :1]
                gate = total[block * rows : (block + 1) * rows, :inner]
                result = total[block * rows : (block + 1) * rows, inner:] * weight
                here = slice((at + block) * rows, (at + block + 1) * rows)
                hidden[here] = (gate / (1.0 + jnp.exp(-gate)) * result).astype(BF16)
        for mask, down in sorted(zip(masks, weights), key=lambda item: item[0]):
            slot = ((mask & ~1) ^ (seq & PAIR)) // 2
            cols = pl.ds(pl.multiple_of(slot * chunk, chunk), chunk)
            for at in range(0, 2 * blocks, 2 * STEP):
                here = hidden[at * rows : (at + 2 * STEP) * rows]
                result = dot(here, down[2 * inner :, :]).astype(BF16)
                for block in range(at, at + 2 * STEP):
                    target = outs[2 * (mask & 1) + block % 2]
                    piece = result[(block - at) * rows : (block - at + 1) * rows]
                    target[block // blocks, block % blocks // 2, :, cols] = piece

    arrays = [array for _, array in parts]
    operands = [place, *own_blocks, *pair_blocks, *arrays, sums]
    shape = jax.ShapeDtypeStruct((2, blocks // 2, rows, width), BF16)
    return pl.pallas_call(
        body,
        out_shape=(shape,) * 4,
        in_specs=[smem()] + [vmem()] * (len(operands) - 1),
        out_specs=(vmem(),) * 4,
        scratch_shapes=[pltpu.VMEM((2 * half, inner), BF16)],
        compiler_params=params(),
        name="expert",
    )(*operands)


def flatten(parts):
    return [array for _, arrays in parts for array in arrays]


def regroup(parts, refs):
    refs = list(refs)
    found = []
    for offset, arrays in parts:
        found.append((offset, refs[: len(arrays)]))
        refs = refs[len(arrays) :]
    return found


def attention_stage(place, table, lengths, latents, w_kv, groups):
    count, _, pages, rows, _ = latents.shape
    width = w_kv.shape[0]
    chunk = width // count
    block_rows = groups[0][1][0][1][0].shape[0]
    tokens = block_rows * count
    prompt = tokens // pages
    lat = rows * count
    keys_all = lat + prompt
    per_block = max(1, min(count, 256 * 1024 // (keys_all * rows)))
    query_rows = per_block * rows
    scale = 1.0 / math.sqrt(HD)
    rate = scale * math.log2(math.e)
    flat = [flatten(parts) for _, parts in groups]

    def body(*refs):
        own, places, used, packed, w_ref = refs[:5]
        rest = list(refs[5:])
        out, grads, mixed, prompt_grad, keys, values, key_grad, value_grad, acc = rest[-9:]
        own_place = places[0, own[1]]
        for (masks, parts), arrays in zip(groups, flat):
            for source, part_refs in regroup(parts, rest[: len(arrays)]):
                owner = places[1, (own_place + source + count) % count]
                place = pl.multiple_of(owner * block_rows, block_rows)
                for index, mask in enumerate(masks):
                    start = pl.multiple_of(((owner & ~PAIR) ^ mask) * chunk, chunk)
                    cols = slice(index * chunk, (index + 1) * chunk)
                    piece = jnp.concatenate([ref[:, cols] for ref in part_refs], axis=0)
                    mixed[pl.ds(place, block_rows), pl.ds(start, chunk)] = piece
            rest = rest[len(arrays) :]
        projected = dot(mixed[...], w_ref[...]).astype(BF16)
        for page in range(pages):
            at = slice(page * prompt, (page + 1) * prompt)
            keys[page, :lat] = packed[:, 1, page].reshape(lat, HD)
            values[page, :lat] = packed[:, 2, page].reshape(lat, HD)
            keys[page, lat:] = projected[at, :HD]
            values[page, lat:] = projected[at, HD:]

        def one_block(step, carry):
            block = pl.ds(step * per_block, per_block)
            for page in range(pages):
                query = packed[block, 0, page].reshape(query_rows, HD)
                grad = packed[block, 3, page].reshape(query_rows, HD)
                key = keys[page]
                value = values[page]
                scores = lax.dot_general(key, query, NT, preferred_element_type=F32)
                position = lax.broadcasted_iota(jnp.int32, (prompt, query_rows), 0)
                used_scores = jnp.where(position < used[page], scores[lat:], -jnp.inf)
                scores = jnp.concatenate([scores[:lat], used_scores], axis=0)
                highest = jnp.max(scores, axis=0, keepdims=True)
                raised = jnp.exp2((scores - highest) * rate)
                soft = raised * (1.0 / jnp.sum(raised, axis=0, keepdims=True))
                low = soft.astype(BF16)
                prob = lax.dot_general(value, grad, NT, preferred_element_type=F32)
                centre = jnp.sum(soft * prob, axis=0, keepdims=True)
                score_grad = (soft * (prob - centre) * scale).astype(BF16)
                attended = lax.dot_general(value, low, TN, preferred_element_type=F32).T
                query_grad = lax.dot_general(key, score_grad, TN, preferred_element_type=F32).T
                out[block, 0, page] = attended.astype(BF16).reshape(per_block, rows, HD)
                out[block, 1, page] = query_grad.astype(BF16).reshape(per_block, rows, HD)
                key_grad[page] += dot(score_grad, query)
                value_grad[page] += dot(low, grad)
            return carry

        key_grad[...] = jnp.zeros(key_grad.shape, F32)
        value_grad[...] = jnp.zeros(value_grad.shape, F32)
        lax.fori_loop(0, count // per_block, one_block, 0)
        for page in range(pages):
            out[:, 2, page] = key_grad[page, :lat].astype(BF16).reshape(count, rows, HD)
            out[:, 3, page] = value_grad[page, :lat].astype(BF16).reshape(count, rows, HD)
            at = slice(page * prompt, (page + 1) * prompt)
            prompt_grad[at, :HD] = key_grad[page, lat:].astype(BF16)
            prompt_grad[at, HD:] = value_grad[page, lat:].astype(BF16)
        total = lax.dot_general(mixed[...], prompt_grad[...], TN, preferred_element_type=F32)
        acc[pl.ds(0, width, stride=2), :] = total[:, :HD]
        acc[pl.ds(1, width, stride=2), :] = total[:, HD:]
        grads[...] = acc[...].astype(BF16)

    operands = [place, table, lengths, latents, w_kv]
    operands += [array for arrays in flat for array in arrays]
    return pl.pallas_call(
        body,
        out_shape=(
            jax.ShapeDtypeStruct(latents.shape, BF16),
            jax.ShapeDtypeStruct((2 * width, HD), BF16),
        ),
        in_specs=[smem()] * 3 + [vmem()] * (len(operands) - 3),
        out_specs=(vmem(),) * 2,
        scratch_shapes=[
            pltpu.VMEM((tokens, width), BF16),
            pltpu.VMEM((tokens, 2 * HD), BF16),
            pltpu.VMEM((pages, keys_all, HD), BF16),
            pltpu.VMEM((pages, keys_all, HD), BF16),
            pltpu.VMEM((pages, keys_all, HD), F32),
            pltpu.VMEM((pages, keys_all, HD), F32),
            pltpu.VMEM((2 * width, HD), F32),
        ],
        compiler_params=params(),
        name="attention",
    )(*operands)


def local(
    prompt_rows,
    expert_ids,
    expert_gates,
    w_gate,
    w_up,
    w_down,
    w_kv,
    prompt_lengths,
    latent_q,
    latent_k,
    latent_v,
    grad_out,
):
    count = lax.axis_size("seq")
    langs = lax.axis_size("lang")
    model_width = prompt_rows.shape[1]
    lang_index = lax.axis_index("lang")
    seq_index = lax.axis_index("seq")
    place = jnp.stack([lang_index, seq_index])
    picks = expert_ids.shape[1]

    packed = pack([latent_q, latent_k, latent_v, grad_out])
    kv_matrix = w_kv.reshape(model_width, 2 * HD)
    along, across, own_blocks, pair_blocks, first, late, sums, (packed, kv_matrix) = gather_inputs(
        w_gate[0].T,
        w_up[0].T,
        w_down[0],
        with_gates(prompt_rows, expert_ids, expert_gates),
        seq_index,
        count,
        (packed, kv_matrix),
        functools.partial(hidden_sums_stage, place),
    )
    packed = tie(packed, late[1][1])
    latents = lax.all_to_all(packed, "seq", split_axis=0, concat_axis=0, tiled=True)

    results = expert_stage(place, own_blocks, pair_blocks, first, late, sums, picks)
    groups = []
    for pair_first, members in enumerate((along, across)):
        keep, send = results[2 * pair_first : 2 * pair_first + 2]
        mixed = reduce_rows(keep, send, bool(pair_first), latents)
        groups.append((sorted(members), ring_gather(mixed, count)))

    out, part = attention_stage(
        place, ring_places(count), prompt_lengths, latents, kv_matrix, groups
    )
    returned = lax.all_to_all(out, "seq", split_axis=0, concat_axis=0, tiled=True)

    mask = langs // 2
    while mask > 1:
        part = (part.astype(F32) + xor_swap(part, "lang", mask).astype(F32)).astype(BF16)
        mask //= 2
    grad_wkv = part.astype(F32) + xor_swap(part, "lang", 1).astype(F32)
    grad_wkv = grad_wkv.reshape(model_width, 2, HD)
    attended, grad_latent = unpack(returned)
    return (attended, grad_latent, grad_wkv)


def solution(mesh):
    return jax.shard_map(
        local,
        mesh=mesh,
        in_specs=(
            P(("lang", "seq"), None),
            P(("lang", "seq"), None),
            P(("lang", "seq"), None),
            P("lang", "seq", None),
            P("lang", "seq", None),
            P("lang", None, "seq"),
            P(None, None, "seq"),
            P("lang"),
            P("lang", "seq", None),
            P("lang", "seq", None),
            P("lang", "seq", None),
            P("lang", "seq", None),
        ),
        out_specs=(P("lang", "seq", None), P(None, "lang", "seq", None), P(None, None, "seq")),
        check_vma=False,
    )
```

profile of v0, /device:TPU:0, one launch (start us, length us, event | category | flops | bytes accessed | tf_op | source)
XLA Modules:
  0.0 217.8 jit_solution(11427286600086308968)
XLA Ops:
  3.1 4.1 %collective-permute-start.1 = (bf16[1056,256]{1,0:T(8,128)(2,1)S(1)}, bf16[1056,256]{1,0:T(8,128)(2,1)S(1)}, u32[]{:S(2)}, u32[]{:S(2)}) collective-permute-start(bf16[1056,256]{1,0:T(8,128)(2,1)S(1)} %pad_maximum_fusion.2.refs_5_.refs_9_), channel_id=1, source_target_pairs={{0,4},{1,5},{2,6},{3,7},{4,0},{5,1},{6,2},{7,3},{8,12},{9,13},{10,... | collective-permute-start | bytes 1622024 | tf_op jit(solution)/shard_map/ppermute | solution.py:76
  8.7 1.6 collective-permute-start.2
  11.5 2.4 %pack.1 = bf16[8,4,2,64,128]{4,3,2,1,0:T(8,128)(2,1)} custom-call(bf16[2,64,1024]{2,1,0:T(8,128)(2,1)} %refs_0_.1, bf16[2,64,1024]{2,1,0:T(8,128)(2,1)} %refs_1_.2, bf16[2,64,1024]{2,1,0:T(8,128)(2,1)} %refs_2_.2, bf16[2,64,1024]{2,1,0:T(8,128)(2,1)} %refs_3_.1), custom_call_target="tpu_custom_call" | custom-call | tf_op jit(solution)/shard_map/pack/pallas_call | solution.py:178
  14.0 18.6 %collective-permute-done.2.refs_7_.refs_11_ = bf16[1056,256]{1,0:T(8,128)(2,1)S(1)} collective-permute-done((bf16[1056,256]{1,0:T(8,128)(2,1)S(1)}, bf16[1056,256]{1,0:T(8,128)(2,1)S(1)}, u32[]{:S(2)}, u32[]{:S(2)}) %collective-permute-start.2) | collective-permute-done | bytes 540704 | tf_op jit(solution)/shard_map/ppermute | solution.py:76
  34.4 2.4 %collective-permute-start.5 = (bf16[1056,256]{1,0:T(8,128)(2,1)S(1)}, bf16[1056,256]{1,0:T(8,128)(2,1)}, u32[]{:S(2)}, u32[]{:S(2)}) collective-permute-start(bf16[1056,256]{1,0:T(8,128)(2,1)S(1)} %pad_maximum_fusion.1), channel_id=1, source_target_pairs={{0,6},{1,7},{2,4},{3,5},{4,2},{5,3},{6,0},{7,1},{8,14},{9,15},{10,... | collective-permute-start | bytes 1622024 | tf_op jit(solution)/shard_map/ppermute | solution.py:76
  38.8 21.1 %collective-permute-done.5.refs_15_ = bf16[1056,256]{1,0:T(8,128)(2,1)} collective-permute-done((bf16[1056,256]{1,0:T(8,128)(2,1)S(1)}, bf16[1056,256]{1,0:T(8,128)(2,1)}, u32[]{:S(2)}, u32[]{:S(2)}) %collective-permute-start.5) | collective-permute-done | bytes 540704 | tf_op jit(solution)/shard_map/ppermute | solution.py:76
  66.0 5.1 %hidden_sums.1.refs_17_ = f32[512,704]{1,0:T(8,128)} custom-call(s32[2]{0:T(128)} %pad_add_fusion.refs_0_, bf16[144,2048]{1,0:T(8,128)(2,1)} %copy-done, bf16[144,2048]{1,0:T(8,128)(2,1)} %copy-done.5, bf16[144,2048]{1,0:T(8,128)(2,1)} %copy-done.4, bf16[144,2048]{1,0:T(8,128)(2,1)} %copy-done.6, bf16[1056,256]{1,0:T(8,128)(2,1)} %copy-done.1, ...), custom_call_target="tpu_custom_call" | custom-call | tf_op jit(solution)/shard_map/hidden_sums/pallas_call | solution.py:254
  71.2 5.6 %collective-permute-done.8.refs_16_ = bf16[1056,256]{1,0:T(8,128)(2,1)S(1)} collective-permute-done((bf16[1056,256]{1,0:T(8,128)(2,1)}, bf16[1056,256]{1,0:T(8,128)(2,1)S(1)}, u32[]{:S(2)}, u32[]{:S(2)}) %collective-permute-start.8) | collective-permute-done | bytes 540704 | tf_op jit(solution)/shard_map/ppermute | solution.py:76
  77.6 3.6 %all-to-all-start = ((bf16[8,4,2,64,128]{4,3,2,1,0:T(8,128)(2,1)}), bf16[8,4,2,64,128]{4,3,2,1,0:T(8,128)(2,1)S(1)}, u32[]{:S(2)}, u32[]{:S(2)}) async-start(bf16[8,4,2,64,128]{4,3,2,1,0:T(8,128)(2,1)} %pack.1), calls=%async_computation | async-start | bytes 2097152 | tf_op jit(solution)/shard_map/all_to_all | solution.py:476
  82.0 11.0 %expert.1 = (bf16[2,2,128,1024]{3,2,1,0:T(8,128)(2,1)}, bf16[2,2,128,1024]{3,2,1,0:T(8,128)(2,1)}, bf16[2,2,128,1024]{3,2,1,0:T(8,128)(2,1)}, bf16[2,2,128,1024]{3,2,1,0:T(8,128)(2,1)}) custom-call(s32[2]{0:T(128)} %pad_add_fusion.refs_0_, bf16[144,2048]{1,0:T(8,128)(2,1)} %copy-done, bf16[144,2048]{1,0:T(8,128)(2,1)} %copy-done.5, ...), custom_call_target="tpu_custom_call" | custom-call | tf_op jit(solution)/shard_map/expert/pallas_call | solution.py:315
  93.6 2.4 %collective-permute-done.14 = bf16[2,2,128,1024]{3,2,1,0:T(8,128)(2,1)S(1)} collective-permute-done((bf16[2,2,128,1024]{3,2,1,0:T(8,128)(2,1)}, bf16[2,2,128,1024]{3,2,1,0:T(8,128)(2,1)S(1)}, u32[]{:S(2)}, u32[]{:S(2)}) %collective-permute-start.14) | collective-permute-done | bytes 1048608 | tf_op jit(solution)/shard_map/ppermute | solution.py:76
  96.1 1.6 convert_add_fusion.2
  102.0 5.8 %all-to-all-done.refs_3_ = bf16[8,4,2,64,128]{4,3,2,1,0:T(8,128)(2,1)S(1)} async-done(((bf16[8,4,2,64,128]{4,3,2,1,0:T(8,128)(2,1)}), bf16[8,4,2,64,128]{4,3,2,1,0:T(8,128)(2,1)S(1)}, u32[]{:S(2)}, u32[]{:S(2)}) %all-to-all-start) | async-done | bytes 1048608 | tf_op jit(solution)/shard_map/all_to_all | solution.py:476
  107.9 5.2 %collective-permute-done.15 = bf16[2,1,128,1024]{3,2,1,0:T(8,128)(2,1)} collective-permute-done((bf16[2,1,128,1024]{3,2,1,0:T(8,128)(2,1)}, bf16[2,1,128,1024]{3,2,1,0:T(8,128)(2,1)}, u32[]{:S(2)}, u32[]{:S(2)}) %collective-permute-start.15) | collective-permute-done | bytes 524320 | tf_op jit(solution)/shard_map/ppermute | solution.py:76
  114.3 1.7 collective-permute-start.16
  116.0 6.9 %collective-permute-done.26 = bf16[2,128,1024]{2,1,0:T(8,128)(2,1)S(1)} collective-permute-done((bf16[2,128,1024]{2,1,0:T(8,128)(2,1)}, bf16[2,128,1024]{2,1,0:T(8,128)(2,1)S(1)}, u32[]{:S(2)}, u32[]{:S(2)}) %collective-permute-start.26) | collective-permute-done | bytes 524320 | tf_op jit(solution)/shard_map/ppermute | solution.py:76
  124.7 2.6 %collective-permute-done.16 = bf16[1,128,1024]{2,1,0:T(8,128)(2,1)S(1)} collective-permute-done((bf16[1,128,1024]{2,1,0:T(8,128)(2,1)S(1)}, bf16[1,128,1024]{2,1,0:T(8,128)(2,1)S(1)}, u32[]{:S(2)}, u32[]{:S(2)}) %collective-permute-start.16) | collective-permute-done | bytes 262176 | tf_op jit(solution)/shard_map/ppermute | solution.py:76
  127.3 1.5 collective-permute-start.18
  129.7 1.5 collective-permute-start.29
  131.8 4.8 %collective-permute-done.18.refs_7_ = bf16[128,1024]{1,0:T(8,128)(2,1)S(1)} collective-permute-done((bf16[128,1024]{1,0:T(8,128)(2,1)S(1)}, bf16[128,1024]{1,0:T(8,128)(2,1)S(1)}, u32[]{:S(2)}, u32[]{:S(2)}) %collective-permute-start.18) | collective-permute-done | bytes 262176 | tf_op jit(solution)/shard_map/ppermute | solution.py:59
  138.7 3.6 %collective-permute-done.29.refs_16_ = bf16[128,1024]{1,0:T(8,128)(2,1)S(1)} collective-permute-done((bf16[128,1024]{1,0:T(8,128)(2,1)S(1)}, bf16[128,1024]{1,0:T(8,128)(2,1)S(1)}, u32[]{:S(2)}, u32[]{:S(2)}) %collective-permute-start.29) | collective-permute-done | bytes 262176 | tf_op jit(solution)/shard_map/ppermute | solution.py:59
  144.3 3.6 %collective-permute-done.20.refs_9_ = bf16[128,1024]{1,0:T(8,128)(2,1)S(1)} collective-permute-done((bf16[128,1024]{1,0:T(8,128)(2,1)S(1)}, bf16[128,1024]{1,0:T(8,128)(2,1)S(1)}, u32[]{:S(2)}, u32[]{:S(2)}) %collective-permute-start.20) | collective-permute-done | bytes 262176 | tf_op jit(solution)/shard_map/ppermute | solution.py:59
  149.9 3.6 %collective-permute-done.31.refs_18_ = bf16[128,1024]{1,0:T(8,128)(2,1)S(1)} collective-permute-done((bf16[128,1024]{1,0:T(8,128)(2,1)S(1)}, bf16[128,1024]{1,0:T(8,128)(2,1)S(1)}, u32[]{:S(2)}, u32[]{:S(2)}) %collective-permute-start.31) | collective-permute-done | bytes 262176 | tf_op jit(solution)/shard_map/ppermute | solution.py:59
  155.5 3.6 %collective-permute-done.22.refs_11_ = bf16[128,1024]{1,0:T(8,128)(2,1)S(1)} collective-permute-done((bf16[128,1024]{1,0:T(8,128)(2,1)S(1)}, bf16[128,1024]{1,0:T(8,128)(2,1)S(1)}, u32[]{:S(2)}, u32[]{:S(2)}) %collective-permute-start.22) | collective-permute-done | bytes 262176 | tf_op jit(solution)/shard_map/ppermute | solution.py:59
  161.3 3.5 %collective-permute-done.33.refs_20_ = bf16[128,1024]{1,0:T(8,128)(2,1)S(1)} collective-permute-done((bf16[128,1024]{1,0:T(8,128)(2,1)S(1)}, bf16[128,1024]{1,0:T(8,128)(2,1)S(1)}, u32[]{:S(2)}, u32[]{:S(2)}) %collective-permute-start.33) | collective-permute-done | bytes 262176 | tf_op jit(solution)/shard_map/ppermute | solution.py:59
  167.9 1.8 collective-permute-done.35.refs_22_
  169.8 1.8 collective-permute-done.34.refs_21_
  171.7 13.1 %attention.1 = (bf16[8,4,2,64,128]{4,3,2,1,0:T(8,128)(2,1)}, bf16[4096,128]{1,0:T(8,128)(2,1)}) custom-call(s32[2]{0:T(128)} %pad_add_fusion.refs_0_, s32[2,8]{1,0:T(2,128)} %constant.56.clone.refs_1_, s32[2]{0:T(128)} %refs_2_.3, bf16[8,4,2,64,128]{4,3,2,1,0:T(8,128)(2,1)} %copy-done.3, bf16[2048,256]{1,0:T(8,128)(2,1)} %bitcast.59, ...), custom_call_target="tpu_custom_call" | custom-call | tf_op jit(solution)/shard_map/attention/pallas_call | solution.py:419
  186.3 3.9 %all-to-all-start.1 = ((bf16[8,4,2,64,128]{4,3,2,1,0:T(8,128)(2,1)}), bf16[8,4,2,64,128]{4,3,2,1,0:T(8,128)(2,1)S(1)}, u32[]{:S(2)}, u32[]{:S(2)}) async-start(bf16[8,4,2,64,128]{4,3,2,1,0:T(8,128)(2,1)} %get-tuple-element.53), calls=%async_computation.1 | async-start | bytes 2097152 | tf_op jit(solution)/shard_map/all_to_all | solution.py:488
  190.2 16.0 %collective-permute-done.36 = bf16[4096,128]{1,0:T(8,128)(2,1)} collective-permute-done((bf16[4096,128]{1,0:T(8,128)(2,1)}, bf16[4096,128]{1,0:T(8,128)(2,1)}, u32[]{:S(2)}, u32[]{:S(2)}) %collective-permute-start.36) | collective-permute-done | bytes 1048608 | tf_op jit(solution)/shard_map/ppermute | solution.py:76
  207.8 5.0 %all-to-all-done.1.packed = bf16[8,4,2,64,128]{4,3,2,1,0:T(8,128)(2,1)S(1)} async-done(((bf16[8,4,2,64,128]{4,3,2,1,0:T(8,128)(2,1)}), bf16[8,4,2,64,128]{4,3,2,1,0:T(8,128)(2,1)S(1)}, u32[]{:S(2)}, u32[]{:S(2)}) %all-to-all-start.1) | async-done | bytes 1048608 | tf_op jit(solution)/shard_map/all_to_all | solution.py:488
  213.8 2.5 %unpack.1 = (bf16[2,64,1024]{2,1,0:T(8,128)(2,1)}, bf16[3,2,64,1024]{3,2,1,0:T(8,128)(2,1)}) custom-call(bf16[8,4,2,64,128]{4,3,2,1,0:T(8,128)(2,1)} %copy-done.2), custom_call_target="tpu_custom_call" | custom-call | tf_op jit(solution)/shard_map/unpack/pallas_call | solution.py:198
  (160 shorter events, 44.9 us)
Async XLA Ops:
  3.1 29.6 %collective-permute-start.1 = (bf16[1056,256]{1,0:T(8,128)(2,1)S(1)}, bf16[1056,256]{1,0:T(8,128)(2,1)S(1)}, u32[]{:S(2)}, u32[]{:S(2)}) collective-permute-start(bf16[1056,256]{1,0:T(8,128)(2,1)S(1)} %pad_maximum_fusion.2.refs_5_.refs_9_), channel_id=1, source_target_pairs={{0,4},{1,5},{2,6},{3,7},{4,0},{5,1},{6,2},{7,3},{8,12},{9,13},{10,... | collective-permute-start | bytes 1622024 | tf_op jit(solution)/shard_map/ppermute | solution.py:76
  7.2 25.5 %collective-permute-start = (bf16[1056,256]{1,0:T(8,128)(2,1)S(1)}, bf16[1056,256]{1,0:T(8,128)(2,1)S(1)}, u32[]{:S(2)}, u32[]{:S(2)}) collective-permute-start(bf16[1056,256]{1,0:T(8,128)(2,1)S(1)} %pad_maximum_fusion.2.refs_5_.refs_9_), channel_id=1, source_target_pairs={{0,1},{1,0},{2,3},{3,2},{4,5},{5,4},{6,7},{7,6},{8,9},{9,8},{10,11... | collective-permute-start | bytes 1622024 | tf_op jit(solution)/shard_map/ppermute | solution.py:76
  8.7 23.9 %collective-permute-start.2 = (bf16[1056,256]{1,0:T(8,128)(2,1)S(1)}, bf16[1056,256]{1,0:T(8,128)(2,1)S(1)}, u32[]{:S(2)}, u32[]{:S(2)}) collective-permute-start(bf16[1056,256]{1,0:T(8,128)(2,1)S(1)} %pad_maximum_fusion.1), channel_id=1, source_target_pairs={{0,2},{1,3},{2,0},{3,1},{4,6},{5,7},{6,4},{7,5},{8,10},{9,11},{10,... | collective-permute-start | bytes 1622024 | tf_op jit(solution)/shard_map/ppermute | solution.py:76
  32.7 28.8 %collective-permute-start.3 = (bf16[144,2048]{1,0:T(8,128)(2,1)S(1)}, bf16[144,2048]{1,0:T(8,128)(2,1)}, u32[]{:S(2)}, u32[]{:S(2)}) collective-permute-start(bf16[144,2048]{1,0:T(8,128)(2,1)S(1)} %pad_maximum_fusion.refs_1_), channel_id=1, source_target_pairs={{0,2},{1,3},{2,0},{3,1},{4,6},{5,7},{6,4},{7,5},{8,10},{9,11},{10,... | collective-permute-start | bytes 1769480 | tf_op jit(solution)/shard_map/ppermute | solution.py:76
  32.9 28.6 %collective-permute-start.4 = (bf16[144,2048]{1,0:T(8,128)(2,1)S(1)}, bf16[144,2048]{1,0:T(8,128)(2,1)S(1)}, u32[]{:S(2)}, u32[]{:S(2)}) collective-permute-start(bf16[144,2048]{1,0:T(8,128)(2,1)S(1)} %pad_maximum_fusion.refs_1_), channel_id=1, source_target_pairs={{0,16},{8,24},{16,0},{24,8},{1,17},{9,25},{17,1},{25,9},{2,18},{10... | collective-permute-start | bytes 1769480 | tf_op jit(solution)/shard_map/ppermute | solution.py:76
  34.4 25.6 %collective-permute-start.5 = (bf16[1056,256]{1,0:T(8,128)(2,1)S(1)}, bf16[1056,256]{1,0:T(8,128)(2,1)}, u32[]{:S(2)}, u32[]{:S(2)}) collective-permute-start(bf16[1056,256]{1,0:T(8,128)(2,1)S(1)} %pad_maximum_fusion.1), channel_id=1, source_target_pairs={{0,6},{1,7},{2,4},{3,5},{4,2},{5,3},{6,0},{7,1},{8,14},{9,15},{10,... | collective-permute-start | bytes 1622024 | tf_op jit(solution)/shard_map/ppermute | solution.py:76
  36.8 23.2 %collective-permute-start.6 = (bf16[1056,256]{1,0:T(8,128)(2,1)S(1)}, bf16[1056,256]{1,0:T(8,128)(2,1)S(1)}, u32[]{:S(2)}, u32[]{:S(2)}) collective-permute-start(bf16[1056,256]{1,0:T(8,128)(2,1)S(1)} %collective-permute-done.1.refs_9_.refs_13_), channel_id=1, source_target_pairs={{0,1},{1,0},{2,3},{3,2},{4,5},{5,4},{6,7},{7,6},{8,9},{9,8},{10,11... | collective-permute-start | bytes 1622024 | tf_op jit(solution)/shard_map/ppermute | solution.py:76
  37.7 23.7 %collective-permute-start.7 = (bf16[1056,256]{1,0:T(8,128)(2,1)S(1)}, bf16[1056,256]{1,0:T(8,128)(2,1)S(1)}, u32[]{:S(2)}, u32[]{:S(2)}) collective-permute-start(bf16[1056,256]{1,0:T(8,128)(2,1)S(1)} %collective-permute-done.2.refs_7_.refs_11_), channel_id=1, source_target_pairs={{0,1},{1,0},{2,3},{3,2},{4,5},{5,4},{6,7},{7,6},{8,9},{9,8},{10,11... | collective-permute-start | bytes 1622024 | tf_op jit(solution)/shard_map/ppermute | solution.py:76
  61.6 16.1 %collective-permute-start.9 = (bf16[144,2048]{1,0:T(8,128)(2,1)}, bf16[144,2048]{1,0:T(8,128)(2,1)}, u32[]{:S(2)}, u32[]{:S(2)}) collective-permute-start(bf16[144,2048]{1,0:T(8,128)(2,1)} %collective-permute-done.3.refs_5_), channel_id=1, source_target_pairs={{0,16},{8,24},{16,0},{24,8},{1,17},{9,25},{17,1},{25,9},{2,18},{10... | collective-permute-start | bytes 1769480 | tf_op jit(solution)/shard_map/ppermute | solution.py:76
  62.3 14.6 %collective-permute-start.8 = (bf16[1056,256]{1,0:T(8,128)(2,1)}, bf16[1056,256]{1,0:T(8,128)(2,1)S(1)}, u32[]{:S(2)}, u32[]{:S(2)}) collective-permute-start(bf16[1056,256]{1,0:T(8,128)(2,1)} %collective-permute-done.5.refs_15_), channel_id=1, source_target_pairs={{0,1},{1,0},{2,3},{3,2},{4,5},{5,4},{6,7},{7,6},{8,9},{9,8},{10,11... | collective-permute-start | bytes 1622024 | tf_op jit(solution)/shard_map/ppermute | solution.py:76
  64.4 16.8 %collective-permute-start.12 = (bf16[144,2048]{1,0:T(8,128)(2,1)}, bf16[144,2048]{1,0:T(8,128)(2,1)}, u32[]{:S(2)}, u32[]{:S(2)}) collective-permute-start(bf16[144,2048]{1,0:T(8,128)(2,1)} %collective-permute-done.3.refs_5_), channel_id=1, source_target_pairs={{0,8},{8,0},{16,24},{24,16},{1,9},{9,1},{17,25},{25,17},{2,10},{10... | collective-permute-start | bytes 1769480 | tf_op jit(solution)/shard_map/ppermute | solution.py:76
  77.6 30.2 %all-to-all-start = ((bf16[8,4,2,64,128]{4,3,2,1,0:T(8,128)(2,1)}), bf16[8,4,2,64,128]{4,3,2,1,0:T(8,128)(2,1)S(1)}, u32[]{:S(2)}, u32[]{:S(2)}) async-start(bf16[8,4,2,64,128]{4,3,2,1,0:T(8,128)(2,1)} %pack.1), calls=%async_computation | async-start | bytes 2097152 | tf_op jit(solution)/shard_map/all_to_all | solution.py:476
  98.6 14.5 %collective-permute-start.15 = (bf16[2,1,128,1024]{3,2,1,0:T(8,128)(2,1)}, bf16[2,1,128,1024]{3,2,1,0:T(8,128)(2,1)}, u32[]{:S(2)}, u32[]{:S(2)}) collective-permute-start(bf16[2,1,128,1024]{3,2,1,0:T(8,128)(2,1)} %pad_maximum_fusion.3), channel_id=1, source_target_pairs={{0,16},{8,24},{16,0},{24,8},{1,17},{9,25},{17,1},{25,9},{2,18},{10... | collective-permute-start | bytes 1572872 | tf_op jit(solution)/shard_map/ppermute | solution.py:76
  107.9 15.0 %collective-permute-start.26 = (bf16[2,128,1024]{2,1,0:T(8,128)(2,1)}, bf16[2,128,1024]{2,1,0:T(8,128)(2,1)S(1)}, u32[]{:S(2)}, u32[]{:S(2)}) collective-permute-start(bf16[2,128,1024]{2,1,0:T(8,128)(2,1)} %fusion), channel_id=1, source_target_pairs={{0,2},{1,3},{2,0},{3,1},{4,6},{5,7},{6,4},{7,5},{8,10},{9,11},{10,... | collective-permute-start | bytes 1572872 | tf_op jit(solution)/shard_map/ppermute | solution.py:76
  114.3 12.9 %collective-permute-start.16 = (bf16[1,128,1024]{2,1,0:T(8,128)(2,1)S(1)}, bf16[1,128,1024]{2,1,0:T(8,128)(2,1)S(1)}, u32[]{:S(2)}, u32[]{:S(2)}) collective-permute-start(bf16[1,128,1024]{2,1,0:T(8,128)(2,1)S(1)} %fusion.7), channel_id=1, source_target_pairs={{0,2},{1,3},{2,0},{3,1},{4,6},{5,7},{6,4},{7,5},{8,10},{9,11},{10,... | collective-permute-start | bytes 786440 | tf_op jit(solution)/shard_map/ppermute | solution.py:76
  127.3 9.3 %collective-permute-start.18 = (bf16[128,1024]{1,0:T(8,128)(2,1)S(1)}, bf16[128,1024]{1,0:T(8,128)(2,1)S(1)}, u32[]{:S(2)}, u32[]{:S(2)}) collective-permute-start(bf16[128,1024]{1,0:T(8,128)(2,1)S(1)} %fusion.6.refs_5_), channel_id=1, source_target_pairs={{0,1},{2,0},{4,2},{6,4},{7,6},{5,7},{3,5},{1,3},{8,9},{10,8},{12,1... | collective-permute-start | bytes 786440 | tf_op jit(solution)/shard_map/ppermute | solution.py:59
  128.9 9.2 %collective-permute-start.17 = (bf16[128,1024]{1,0:T(8,128)(2,1)S(1)}, bf16[128,1024]{1,0:T(8,128)(2,1)S(1)}, u32[]{:S(2)}, u32[]{:S(2)}) collective-permute-start(bf16[128,1024]{1,0:T(8,128)(2,1)S(1)} %fusion.6.refs_5_), channel_id=1, source_target_pairs={{0,2},{2,4},{4,6},{6,7},{7,5},{5,3},{3,1},{1,0},{8,10},{10,12},{12... | collective-permute-start | bytes 786440 | tf_op jit(solution)/shard_map/ppermute | solution.py:58
  129.7 12.5 %collective-permute-start.29 = (bf16[128,1024]{1,0:T(8,128)(2,1)S(1)}, bf16[128,1024]{1,0:T(8,128)(2,1)S(1)}, u32[]{:S(2)}, u32[]{:S(2)}) collective-permute-start(bf16[128,1024]{1,0:T(8,128)(2,1)S(1)} %fusion.8.refs_14_), channel_id=1, source_target_pairs={{0,1},{2,0},{4,2},{6,4},{7,6},{5,7},{3,5},{1,3},{8,9},{10,8},{12,1... | collective-permute-start | bytes 786440 | tf_op jit(solution)/shard_map/ppermute | solution.py:59
  131.2 12.5 %collective-permute-start.28 = (bf16[128,1024]{1,0:T(8,128)(2,1)S(1)}, bf16[128,1024]{1,0:T(8,128)(2,1)S(1)}, u32[]{:S(2)}, u32[]{:S(2)}) collective-permute-start(bf16[128,1024]{1,0:T(8,128)(2,1)S(1)} %fusion.8.refs_14_), channel_id=1, source_target_pairs={{0,2},{2,4},{4,6},{6,7},{7,5},{5,3},{3,1},{1,0},{8,10},{10,12},{12... | collective-permute-start | bytes 786440 | tf_op jit(solution)/shard_map/ppermute | solution.py:58
  136.6 11.2 %collective-permute-start.20 = (bf16[128,1024]{1,0:T(8,128)(2,1)S(1)}, bf16[128,1024]{1,0:T(8,128)(2,1)S(1)}, u32[]{:S(2)}, u32[]{:S(2)}) collective-permute-start(bf16[128,1024]{1,0:T(8,128)(2,1)S(1)} %collective-permute-done.18.refs_7_), channel_id=1, source_target_pairs={{0,1},{2,0},{4,2},{6,4},{7,6},{5,7},{3,5},{1,3},{8,9},{10,8},{12,1... | collective-permute-start | bytes 786440 | tf_op jit(solution)/shard_map/ppermute | solution.py:59
  138.1 11.2 %collective-permute-start.19 = (bf16[128,1024]{1,0:T(8,128)(2,1)S(1)}, bf16[128,1024]{1,0:T(8,128)(2,1)S(1)}, u32[]{:S(2)}, u32[]{:S(2)}) collective-permute-start(bf16[128,1024]{1,0:T(8,128)(2,1)S(1)} %collective-permute-done.17.refs_6_), channel_id=1, source_target_pairs={{0,2},{2,4},{4,6},{6,7},{7,5},{5,3},{3,1},{1,0},{8,10},{10,12},{12... | collective-permute-start | bytes 786440 | tf_op jit(solution)/shard_map/ppermute | solution.py:58
  142.3 11.2 %collective-permute-start.31 = (bf16[128,1024]{1,0:T(8,128)(2,1)S(1)}, bf16[128,1024]{1,0:T(8,128)(2,1)S(1)}, u32[]{:S(2)}, u32[]{:S(2)}) collective-permute-start(bf16[128,1024]{1,0:T(8,128)(2,1)S(1)} %collective-permute-done.29.refs_16_), channel_id=1, source_target_pairs={{0,1},{2,0},{4,2},{6,4},{7,6},{5,7},{3,5},{1,3},{8,9},{10,8},{12,1... | collective-permute-start | bytes 786440 | tf_op jit(solution)/shard_map/ppermute | solution.py:59
  143.7 11.2 %collective-permute-start.30 = (bf16[128,1024]{1,0:T(8,128)(2,1)S(1)}, bf16[128,1024]{1,0:T(8,128)(2,1)S(1)}, u32[]{:S(2)}, u32[]{:S(2)}) collective-permute-start(bf16[128,1024]{1,0:T(8,128)(2,1)S(1)} %collective-permute-done.28.refs_15_), channel_id=1, source_target_pairs={{0,2},{2,4},{4,6},{6,7},{7,5},{5,3},{3,1},{1,0},{8,10},{10,12},{12... | collective-permute-start | bytes 786440 | tf_op jit(solution)/shard_map/ppermute | solution.py:58
  147.9 11.2 %collective-permute-start.22 = (bf16[128,1024]{1,0:T(8,128)(2,1)S(1)}, bf16[128,1024]{1,0:T(8,128)(2,1)S(1)}, u32[]{:S(2)}, u32[]{:S(2)}) collective-permute-start(bf16[128,1024]{1,0:T(8,128)(2,1)S(1)} %collective-permute-done.20.refs_9_), channel_id=1, source_target_pairs={{0,1},{2,0},{4,2},{6,4},{7,6},{5,7},{3,5},{1,3},{8,9},{10,8},{12,1... | collective-permute-start | bytes 786440 | tf_op jit(solution)/shard_map/ppermute | solution.py:59
  149.4 11.3 %collective-permute-start.21 = (bf16[128,1024]{1,0:T(8,128)(2,1)S(1)}, bf16[128,1024]{1,0:T(8,128)(2,1)S(1)}, u32[]{:S(2)}, u32[]{:S(2)}) collective-permute-start(bf16[128,1024]{1,0:T(8,128)(2,1)S(1)} %collective-permute-done.19.refs_8_), channel_id=1, source_target_pairs={{0,2},{2,4},{4,6},{6,7},{7,5},{5,3},{3,1},{1,0},{8,10},{10,12},{12... | collective-permute-start | bytes 786440 | tf_op jit(solution)/shard_map/ppermute | solution.py:58
  153.5 11.2 %collective-permute-start.33 = (bf16[128,1024]{1,0:T(8,128)(2,1)S(1)}, bf16[128,1024]{1,0:T(8,128)(2,1)S(1)}, u32[]{:S(2)}, u32[]{:S(2)}) collective-permute-start(bf16[128,1024]{1,0:T(8,128)(2,1)S(1)} %collective-permute-done.31.refs_18_), channel_id=1, source_target_pairs={{0,1},{2,0},{4,2},{6,4},{7,6},{5,7},{3,5},{1,3},{8,9},{10,8},{12,1... | collective-permute-start | bytes 786440 | tf_op jit(solution)/shard_map/ppermute | solution.py:59
  155.0 11.3 %collective-permute-start.32 = (bf16[128,1024]{1,0:T(8,128)(2,1)S(1)}, bf16[128,1024]{1,0:T(8,128)(2,1)S(1)}, u32[]{:S(2)}, u32[]{:S(2)}) collective-permute-start(bf16[128,1024]{1,0:T(8,128)(2,1)S(1)} %collective-permute-done.30.refs_17_), channel_id=1, source_target_pairs={{0,2},{2,4},{4,6},{6,7},{7,5},{5,3},{3,1},{1,0},{8,10},{10,12},{12... | collective-permute-start | bytes 786440 | tf_op jit(solution)/shard_map/ppermute | solution.py:58
  159.1 8.0 %collective-permute-start.24 = (bf16[64,1024]{1,0:T(8,128)(2,1)S(1)}, bf16[64,1024]{1,0:T(8,128)(2,1)S(1)}, u32[]{:S(2)}, u32[]{:S(2)}) collective-permute-start(bf16[64,1024]{1,0:T(8,128)(2,1)S(1)} %slice.102), channel_id=1, source_target_pairs={{0,1},{2,0},{4,2},{6,4},{7,6},{5,7},{3,5},{1,3},{8,9},{10,8},{12,1... | collective-permute-start | bytes 393224 | tf_op jit(solution)/shard_map/ppermute | solution.py:63
  160.7 7.3 %collective-permute-start.23 = (bf16[64,1024]{1,0:T(8,128)(2,1)S(1)}, bf16[64,1024]{1,0:T(8,128)(2,1)S(1)}, u32[]{:S(2)}, u32[]{:S(2)}) collective-permute-start(bf16[64,1024]{1,0:T(8,128)(2,1)S(1)} %slice.101), channel_id=1, source_target_pairs={{0,2},{2,4},{4,6},{6,7},{7,5},{5,3},{3,1},{1,0},{8,10},{10,12},{12... | collective-permute-start | bytes 393224 | tf_op jit(solution)/shard_map/ppermute | solution.py:62
  184.8 21.4 %collective-permute-start.36 = (bf16[4096,128]{1,0:T(8,128)(2,1)}, bf16[4096,128]{1,0:T(8,128)(2,1)}, u32[]{:S(2)}, u32[]{:S(2)}) collective-permute-start(bf16[4096,128]{1,0:T(8,128)(2,1)} %get-tuple-element.56), channel_id=1, source_target_pairs={{0,16},{8,24},{16,0},{24,8},{1,17},{9,25},{17,1},{25,9},{2,18},{10... | collective-permute-start | bytes 3145736 | tf_op jit(solution)/shard_map/ppermute | solution.py:76
  186.3 26.5 %all-to-all-start.1 = ((bf16[8,4,2,64,128]{4,3,2,1,0:T(8,128)(2,1)}), bf16[8,4,2,64,128]{4,3,2,1,0:T(8,128)(2,1)S(1)}, u32[]{:S(2)}, u32[]{:S(2)}) async-start(bf16[8,4,2,64,128]{4,3,2,1,0:T(8,128)(2,1)} %get-tuple-element.53), calls=%async_computation.1 | async-start | bytes 2097152 | tf_op jit(solution)/shard_map/all_to_all | solution.py:488
  207.7 8.5 %collective-permute-start.37 = (bf16[4096,128]{1,0:T(8,128)(2,1)S(1)}, bf16[4096,128]{1,0:T(8,128)(2,1)S(1)}, u32[]{:S(2)}, u32[]{:S(2)}) collective-permute-start(bf16[4096,128]{1,0:T(8,128)(2,1)S(1)} %add_convert_fusion), channel_id=1, source_target_pairs={{0,8},{8,0},{16,24},{24,16},{1,9},{9,1},{17,25},{25,17},{2,10},{10... | collective-permute-start | bytes 3145736 | tf_op jit(solution)/shard_map/ppermute | solution.py:76
  (48 other events, 621.0 us)
where the time goes:
time: 218 us
  waiting for transfers between devices  118 us (54%)
  starting transfers between devices  46.4 us (21%)
  Pallas kernels  34.1 us (16%)
  local copies, waits for them, and re-layouts  8.91 us (4%)
  other arithmetic  8.87 us (4%)
    ppermute x22, waiting for transfers between devices, xor_swap(): return lax.ppermute(array, axis, [(i, i ^ mask) for i in range(count)])  80.3 us
    ppermute x6, waiting for transfers between devices, ring_gather(): down = lax.ppermute(down, 'seq', back)  22.6 us
    ppermute x22, starting transfers between devices, xor_swap(): return lax.ppermute(array, axis, [(i, i ^ mask) for i in range(count)])  22.3 us
    pallas_call x1, Pallas kernels, attention_stage(): pl.pallas_call(body, out_shape=(jax.ShapeDtypeStruct(latents.shape, BF16)...  13.1 us
    pallas_call x1, Pallas kernels, expert_stage(): pl.pallas_call(body, out_shape=(shape,) * 4, in_specs=[smem()] + [vmem()]...  11 us
    ppermute x6, starting transfers between devices, ring_gather(): down = lax.ppermute(down, 'seq', back)  8.95 us
    unnamed x81, local copies, waits for them, and re-layouts  6.49 us
    all_to_all x1, waiting for transfers between devices, local(): lax.all_to_all(packed, 'seq', split_axis=0, concat_axis=0, tiled=True)  5.84 us
  transfers between devices with their start and end apart: 40, of which 21 were waited for; matrix products, arithmetic and copies ran while one was open for 4% of the time, Pallas kernels for 10%

commit v1 on v0

--- a/solution.py
+++ b/solution.py
@@ -90,23 +90,24 @@
 def reduce_rows(keep, send, pair_first, after):
     langs = lax.axis_size("lang")
 
-    def over_pair(parts):
-        kept, sent = parts
-        arrived = xor_swap(tie(sent.astype(BF16), after), "seq", PAIR)
-        return kept + arrived.astype(F32)
-
-    arrived = xor_swap(send, "lang", 1)
-    halves = [keep[side].astype(F32) + arrived[side].astype(F32) for side in range(2)]
+    def total(terms):
+        return functools.reduce(lambda a, b: a + b, [term.astype(F32) for term in terms])
+
+    def over_pair(terms):
+        sent = tie(total([term[1:] for term in terms]).astype(BF16), after)
+        return [term[:1] for term in terms] + [xor_swap(sent, "seq", PAIR)]
+
+    terms = [keep, xor_swap(send, "lang", 1)]
     if pair_first:
-        halves = [over_pair(halves)]
+        terms = over_pair(terms)
     mask = 2
     while mask < langs:
-        sent = jnp.stack([half[1::2] for half in halves]).astype(BF16)
-        arrived = xor_swap(sent, "lang", mask).astype(F32)
-        halves = [half[0::2] + arrived[side] for side, half in enumerate(halves)]
+        sent = total([term[:, 1::2] for term in terms]).astype(BF16)
+        terms = [term[:, 0::2] for term in terms] + [xor_swap(sent, "lang", mask)]
         mask *= 2
-    total = halves[0] if pair_first else over_pair(halves)
-    return total[0].astype(BF16)
+    if not pair_first:
+        terms = over_pair(terms)
+    return total(terms)[0, 0].astype(BF16)
 
 
 def split_halves(block, seq_index):
@@ -336,101 +337,122 @@
     return found
 
 
-def attention_stage(place, table, lengths, latents, w_kv, groups):
-    count, _, pages, rows, _ = latents.shape
+def attention_stage(place, table, lengths, latents, w_kv, groups, before=None):
+    count, kinds, pages, rows, _ = latents.shape
     width = w_kv.shape[0]
     chunk = width // count
+    near = count // pages
     block_rows = groups[0][1][0][1][0].shape[0]
-    tokens = block_rows * count
-    prompt = tokens // pages
+    prompt = block_rows * near
     lat = rows * count
     keys_all = lat + prompt
     per_block = max(1, min(count, 256 * 1024 // (keys_all * rows)))
     query_rows = per_block * rows
     scale = 1.0 / math.sqrt(HD)
     rate = scale * math.log2(math.e)
+    skipped = count // 2 if before is None else 0
+    groups = [
+        (masks, [part for part in parts if part[0] != skipped]) for masks, parts in groups
+    ]
     flat = [flatten(parts) for _, parts in groups]
+    old = [] if before is None else list(before)
 
     def body(*refs):
         own, places, used, packed, w_ref = refs[:5]
-        rest = list(refs[5:])
+        old_refs = refs[5 : 5 + len(old)]
+        rest = list(refs[5 + len(old) :])
         out, grads, mixed, prompt_grad, keys, values, key_grad, value_grad, acc = rest[-9:]
         own_place = places[0, own[1]]
+        page = own[1] // near
+        if old:
+            page = pages - 1 - page
+            out[:, :, own[1] // near] = old_refs[0][...]
         for (masks, parts), arrays in zip(groups, flat):
             for source, part_refs in regroup(parts, rest[: len(arrays)]):
                 owner = places[1, (own_place + source + count) % count]
-                place = pl.multiple_of(owner * block_rows, block_rows)
-                for index, mask in enumerate(masks):
-                    start = pl.multiple_of(((owner & ~PAIR) ^ mask) * chunk, chunk)
-                    cols = slice(index * chunk, (index + 1) * chunk)
-                    piece = jnp.concatenate([ref[:, cols] for ref in part_refs], axis=0)
-                    mixed[pl.ds(place, block_rows), pl.ds(start, chunk)] = piece
+                at = pl.multiple_of(owner % near * block_rows, block_rows)
+
+                @pl.when(owner // near == page)
+                def _(masks=masks, part_refs=part_refs, owner=owner, at=at):
+                    for index, mask in enumerate(masks):
+                        start = pl.multiple_of(((owner & ~PAIR) ^ mask) * chunk, chunk)
+                        cols = slice(index * chunk, (index + 1) * chunk)
+                        piece = jnp.concatenate([ref[:, cols] for ref in part_refs], axis=0)
+                        mixed[pl.ds(at, block_rows), pl.ds(start, chunk)] = piece
+
             rest = rest[len(arrays) :]
         projected = dot(mixed[...], w_ref[...]).astype(BF16)
-        for page in range(pages):
-            at = slice(page * prompt, (page + 1) * prompt)
-            keys[page, :lat] = packed[:, 1, page].reshape(lat, HD)
-            values[page, :lat] = packed[:, 2, page].reshape(lat, HD)
-            keys[page, lat:] = projected[at, :HD]
-            values[page, lat:] = projected[at, HD:]
+        keys[:lat] = packed[:, 1, page].reshape(lat, HD)
+        values[:lat] = packed[:, 2, page].reshape(lat, HD)
+        keys[lat:] = projected[:, :HD]
+        values[lat:] = projected[:, HD:]
+        key_grad[...] = jnp.zeros(key_grad.shape, F32)
+        value_grad[...] = jnp.zeros(value_grad.shape, F32)
+        target = out.at[:, :, page] if old else out
 
         def one_block(step, carry):
             block = pl.ds(step * per_block, per_block)
-            for page in range(pages):
-                query = packed[block, 0, page].reshape(query_rows, HD)
-                grad = packed[block, 3, page].reshape(query_rows, HD)
-                key = keys[page]
-                value = values[page]
-                scores = lax.dot_general(key, query, NT, preferred_element_type=F32)
-                position = lax.broadcasted_iota(jnp.int32, (prompt, query_rows), 0)
-                used_scores = jnp.where(position < used[page], scores[lat:], -jnp.inf)
-                scores = jnp.concatenate([scores[:lat], used_scores], axis=0)
-                highest = jnp.max(scores, axis=0, keepdims=True)
-                raised = jnp.exp2((scores - highest) * rate)
-                soft = raised * (1.0 / jnp.sum(raised, axis=0, keepdims=True))
-                low = soft.astype(BF16)
-                prob = lax.dot_general(value, grad, NT, preferred_element_type=F32)
-                centre = jnp.sum(soft * prob, axis=0, keepdims=True)
-                score_grad = (soft * (prob - centre) * scale).astype(BF16)
-                attended = lax.dot_general(value, low, TN, preferred_element_type=F32).T
-                query_grad = lax.dot_general(key, score_grad, TN, preferred_element_type=F32).T
-                out[block, 0, page] = attended.astype(BF16).reshape(per_block, rows, HD)
-                out[block, 1, page] = query_grad.astype(BF16).reshape(per_block, rows, HD)
-                key_grad[page] += dot(score_grad, query)
-                value_grad[page] += dot(low, grad)
+            query = packed[block, 0, page].reshape(query_rows, HD)
+            grad = packed[block, 3, page].reshape(query_rows, HD)
+            key = keys[...]
+            value = values[...]
+            scores = lax.dot_general(key, query, NT, preferred_element_type=F32)
+            position = lax.broadcasted_iota(jnp.int32, (prompt, query_rows), 0)
+            used_scores = jnp.where(position < used[page], scores[lat:], -jnp.inf)
+            scores = jnp.concatenate([scores[:lat], used_scores], axis=0)
+            highest = jnp.max(scores, axis=0, keepdims=True)
+            raised = jnp.exp2((scores - highest) * rate)
+            soft = raised * (1.0 / jnp.sum(raised, axis=0, keepdims=True))
+            low = soft.astype(BF16)
+            prob = lax.dot_general(value, grad, NT, preferred_element_type=F32)
+            centre = jnp.sum(soft * prob, axis=0, keepdims=True)
+            score_grad = (soft * (prob - centre) * scale).astype(BF16)
+            attended = lax.dot_general(value, low, TN, preferred_element_type=F32).T
+            query_grad = lax.dot_general(key, score_grad, TN, preferred_element_type=F32).T
+            target[block, 0] = attended.astype(BF16).reshape(per_block, rows, HD)
+            target[block, 1] = query_grad.astype(BF16).reshape(per_block, rows, HD)
+            key_grad[...] += dot(score_grad, query)
+            value_grad[...] += dot(low, grad)
             return carry
 
-        key_grad[...] = jnp.zeros(key_grad.shape, F32)
-        value_grad[...] = jnp.zeros(value_grad.shape, F32)
-        lax.fori_loop(0, count // per_block, one_block, 0)
-        for page in range(pages):
-            out[:, 2, page] = key_grad[page, :lat].astype(BF16).reshape(count, rows, HD)
-            out[:, 3, page] = value_grad[page, :lat].astype(BF16).reshape(count, rows, HD)
-            at = slice(page * prompt, (page + 1) * prompt)
-            prompt_grad[at, :HD] = key_grad[page, lat:].astype(BF16)
-            prompt_grad[at, HD:] = value_grad[page, lat:].astype(BF16)
+        lax.fori_loop(0, count // per_block, one_block, 0, unroll=2)
+        target[:, 2] = key_grad[:lat].astype(BF16).reshape(count, rows, HD)
+        target[:, 3] = value_grad[:lat].astype(BF16).reshape(count, rows, HD)
+        prompt_grad[:, :HD] = key_grad[lat:].astype(BF16)
+        prompt_grad[:, HD:] = value_grad[lat:].astype(BF16)
         total = lax.dot_general(mixed[...], prompt_grad[...], TN, preferred_element_type=F32)
-        acc[pl.ds(0, width, stride=2), :] = total[:, :HD]
-        acc[pl.ds(1, width, stride=2), :] = total[:, HD:]
-        grads[...] = acc[...].astype(BF16)
-
-    operands = [place, table, lengths, latents, w_kv]
+        if old:
+            total = total + old_refs[1][...]
+            acc[pl.ds(0, width, stride=2), :] = total[:, :HD]
+            acc[pl.ds(1, width, stride=2), :] = total[:, HD:]
+            grads[...] = acc[...].astype(BF16)
+        else:
+            grads[...] = total
+
+    operands = [place, table, lengths, latents, w_kv, *old]
     operands += [array for arrays in flat for array in arrays]
+    if old:
+        out_shape = (
+            jax.ShapeDtypeStruct(latents.shape, BF16),
+            jax.ShapeDtypeStruct((2 * width, HD), BF16),
+        )
+    else:
+        out_shape = (
+            jax.ShapeDtypeStruct((count, kinds, rows, HD), BF16),
+            jax.ShapeDtypeStruct((width, 2 * HD), F32),
+        )
     return pl.pallas_call(
         body,
-        out_shape=(
-            jax.ShapeDtypeStruct(latents.shape, BF16),
-            jax.ShapeDtypeStruct((2 * width, HD), BF16),
-        ),
+        out_shape=out_shape,
         in_specs=[smem()] * 3 + [vmem()] * (len(operands) - 3),
         out_specs=(vmem(),) * 2,
         scratch_shapes=[
-            pltpu.VMEM((tokens, width), BF16),
-            pltpu.VMEM((tokens, 2 * HD), BF16),
-            pltpu.VMEM((pages, keys_all, HD), BF16),
-            pltpu.VMEM((pages, keys_all, HD), BF16),
-            pltpu.VMEM((pages, keys_all, HD), F32),
-            pltpu.VMEM((pages, keys_all, HD), F32),
+            pltpu.VMEM((prompt, width), BF16),
+            pltpu.VMEM((prompt, 2 * HD), BF16),
+            pltpu.VMEM((keys_all, HD), BF16),
+            pltpu.VMEM((keys_all, HD), BF16),
+            pltpu.VMEM((keys_all, HD), F32),
+            pltpu.VMEM((keys_all, HD), F32),
             pltpu.VMEM((2 * width, HD), F32),
         ],
         compiler_params=params(),
@@ -482,8 +504,10 @@
         mixed = reduce_rows(keep, send, bool(pair_first), latents)
         groups.append((sorted(members), ring_gather(mixed, count)))
 
+    table = ring_places(count)
+    own_page = attention_stage(place, table, prompt_lengths, latents, kv_matrix, groups)
     out, part = attention_stage(
-        place, ring_places(count), prompt_lengths, latents, kv_matrix, groups
+        place, table, prompt_lengths, latents, kv_matrix, groups, own_page
     )
     returned = lax.all_to_all(out, "seq", split_axis=0, concat_axis=0, tiled=True)
 

time: 218 us -> 222 us (1.018)
  Pallas kernels: 34.1 us -> 40.5 us
  waiting for transfers between devices: 118 us -> 113 us
    pallas_call x1 -> x2, Pallas kernels: 13.1 us -> 19.5 us  [attention_stage(): pl.pallas_call(body, out_shape=out_shape, in_specs=[smem()] * 3 + [vmem()...]
    convert_element_type x5 -> x6, other arithmetic: 2.36 us -> 6.03 us  [the longest x2 2.51 us: reduce_rows(): sent = total([term[:, 1::2] for term in terms]).astype(BF16)]
    ppermute x2, waiting for transfers between devices: 2.69 us -> 0.01 us  [ring_gather(): last_up = lax.ppermute(up[:half_rows], 'seq', ahead)]
    unnamed x81 -> x85, local copies, waits for them, and re-layouts: 6.49 us -> 7.18 us
  transfers between devices with their start and end apart: 40 -> 40, of which waited for: 21 -> 17; matrix products, arithmetic and copies ran while one was open for 4% -> 5% of each run, Pallas kernels for 10% -> 14%
where the time goes in v1:
time: 222 us; the launch traced here: 221 us
  waiting for transfers between devices  113 us (51%)
  starting transfers between devices  46.4 us (21%)
  Pallas kernels  40.5 us (18%)
  local copies, waits for them, and re-layouts  10.2 us (5%)
  other arithmetic  9.79 us (4%)
    ppermute x22, waiting for transfers between devices, xor_swap(): return lax.ppermute(array, axis, [(i, i ^ mask) for i in range(count)])  79.5 us
    ppermute x6, waiting for transfers between devices, ring_gather(): down = lax.ppermute(down, 'seq', back)  22.7 us
    ppermute x22, starting transfers between devices, xor_swap(): return lax.ppermute(array, axis, [(i, i ^ mask) for i in range(count)])  22.4 us
    pallas_call x2, Pallas kernels, attention_stage(): pl.pallas_call(body, out_shape=out_shape, in_specs=[smem()] * 3 + [vmem()...  19.5 us
    pallas_call x1, Pallas kernels, expert_stage(): pl.pallas_call(body, out_shape=(shape,) * 4, in_specs=[smem()] + [vmem()]...  11 us
    ppermute x6, starting transfers between devices, ring_gather(): down = lax.ppermute(down, 'seq', back)  8.95 us
    unnamed x85, local copies, waits for them, and re-layouts  7.18 us
    all_to_all x1, waiting for transfers between devices, local(): lax.all_to_all(packed, 'seq', split_axis=0, concat_axis=0, tiled=True)  5.94 us
  transfers between devices with their start and end apart: 40, of which 17 were waited for; matrix products, arithmetic and copies ran while one was open for 5% of the time, Pallas kernels for 14%

profile of v1, /device:TPU:0, one launch (start us, length us, event | category | flops | bytes accessed | tf_op | source)
XLA Modules:
  0.0 221.3 jit_solution(2859016052717065796)
XLA Ops:
  3.1 4.1 %collective-permute-start.1 = (bf16[1056,256]{1,0:T(8,128)(2,1)S(1)}, bf16[1056,256]{1,0:T(8,128)(2,1)S(1)}, u32[]{:S(2)}, u32[]{:S(2)}) collective-permute-start(bf16[1056,256]{1,0:T(8,128)(2,1)S(1)} %pad_maximum_fusion.2.refs_5_.refs_9_), channel_id=1, source_target_pairs={{0,4},{1,5},{2,6},{3,7},{4,0},{5,1},{6,2},{7,3},{8,12},{9,13},{10,... | collective-permute-start | bytes 1622024 | tf_op jit(solution)/shard_map/ppermute | solution.py:76
  8.7 1.6 collective-permute-start.2
  11.5 2.4 %pack.1 = bf16[8,4,2,64,128]{4,3,2,1,0:T(8,128)(2,1)} custom-call(bf16[2,64,1024]{2,1,0:T(8,128)(2,1)} %refs_0_.1, bf16[2,64,1024]{2,1,0:T(8,128)(2,1)} %refs_1_.3, bf16[2,64,1024]{2,1,0:T(8,128)(2,1)} %refs_2_.3, bf16[2,64,1024]{2,1,0:T(8,128)(2,1)} %refs_3_.1), custom_call_target="tpu_custom_call" | custom-call | tf_op jit(solution)/shard_map/pack/pallas_call | solution.py:179
  14.0 18.7 %collective-permute-done.2.refs_7_.refs_11_ = bf16[1056,256]{1,0:T(8,128)(2,1)S(1)} collective-permute-done((bf16[1056,256]{1,0:T(8,128)(2,1)S(1)}, bf16[1056,256]{1,0:T(8,128)(2,1)S(1)}, u32[]{:S(2)}, u32[]{:S(2)}) %collective-permute-start.2) | collective-permute-done | bytes 540704 | tf_op jit(solution)/shard_map/ppermute | solution.py:76
  34.4 2.4 %collective-permute-start.5 = (bf16[1056,256]{1,0:T(8,128)(2,1)S(1)}, bf16[1056,256]{1,0:T(8,128)(2,1)}, u32[]{:S(2)}, u32[]{:S(2)}) collective-permute-start(bf16[1056,256]{1,0:T(8,128)(2,1)S(1)} %pad_maximum_fusion.1), channel_id=1, source_target_pairs={{0,6},{1,7},{2,4},{3,5},{4,2},{5,3},{6,0},{7,1},{8,14},{9,15},{10,... | collective-permute-start | bytes 1622024 | tf_op jit(solution)/shard_map/ppermute | solution.py:76
  38.8 21.1 %collective-permute-done.5.refs_15_ = bf16[1056,256]{1,0:T(8,128)(2,1)} collective-permute-done((bf16[1056,256]{1,0:T(8,128)(2,1)S(1)}, bf16[1056,256]{1,0:T(8,128)(2,1)}, u32[]{:S(2)}, u32[]{:S(2)}) %collective-permute-start.5) | collective-permute-done | bytes 540704 | tf_op jit(solution)/shard_map/ppermute | solution.py:76
  66.0 5.2 %hidden_sums.1.refs_17_ = f32[512,704]{1,0:T(8,128)} custom-call(s32[2]{0:T(128)} %pad_add_fusion.refs_0_, bf16[144,2048]{1,0:T(8,128)(2,1)} %copy-done.1, bf16[144,2048]{1,0:T(8,128)(2,1)} %copy-done.5, bf16[144,2048]{1,0:T(8,128)(2,1)} %copy-done.4, bf16[144,2048]{1,0:T(8,128)(2,1)} %copy-done.6, bf16[1056,256]{1,0:T(8,128)(2,1)} %copy-done.2, ...), custom_call_target="tpu_custom_call" | custom-call | tf_op jit(solution)/shard_map/hidden_sums/pallas_call | solution.py:255
  71.1 5.7 %collective-permute-done.8.refs_16_ = bf16[1056,256]{1,0:T(8,128)(2,1)S(1)} collective-permute-done((bf16[1056,256]{1,0:T(8,128)(2,1)}, bf16[1056,256]{1,0:T(8,128)(2,1)S(1)}, u32[]{:S(2)}, u32[]{:S(2)}) %collective-permute-start.8) | collective-permute-done | bytes 540704 | tf_op jit(solution)/shard_map/ppermute | solution.py:76
  77.6 3.6 %all-to-all-start = ((bf16[8,4,2,64,128]{4,3,2,1,0:T(8,128)(2,1)}), bf16[8,4,2,64,128]{4,3,2,1,0:T(8,128)(2,1)S(1)}, u32[]{:S(2)}, u32[]{:S(2)}) async-start(bf16[8,4,2,64,128]{4,3,2,1,0:T(8,128)(2,1)} %pack.1), calls=%async_computation | async-start | bytes 2097152 | tf_op jit(solution)/shard_map/all_to_all | solution.py:498
  82.1 11.0 %expert.1 = (bf16[2,2,128,1024]{3,2,1,0:T(8,128)(2,1)}, bf16[2,2,128,1024]{3,2,1,0:T(8,128)(2,1)}, bf16[2,2,128,1024]{3,2,1,0:T(8,128)(2,1)}, bf16[2,2,128,1024]{3,2,1,0:T(8,128)(2,1)}) custom-call(s32[2]{0:T(128)} %pad_add_fusion.refs_0_, bf16[144,2048]{1,0:T(8,128)(2,1)} %copy-done.1, bf16[144,2048]{1,0:T(8,128)(2,1)} %copy-done.5, ...), custom_call_target="tpu_custom_call" | custom-call | tf_op jit(solution)/shard_map/expert/pallas_call | solution.py:316
  93.7 2.4 %collective-permute-done.14 = bf16[2,2,128,1024]{3,2,1,0:T(8,128)(2,1)S(1)} collective-permute-done((bf16[2,2,128,1024]{3,2,1,0:T(8,128)(2,1)}, bf16[2,2,128,1024]{3,2,1,0:T(8,128)(2,1)S(1)}, u32[]{:S(2)}, u32[]{:S(2)}) %collective-permute-start.14) | collective-permute-done | bytes 1048608 | tf_op jit(solution)/shard_map/ppermute | solution.py:76
  96.1 2.4 %add_convert_fusion.2 = bf16[2,1,128,1024]{3,2,1,0:T(8,128)(2,1)} fusion(bf16[2,2,128,1024]{3,2,1,0:T(8,128)(2,1)S(1)} %collective-permute-done.14, bf16[2,2,128,1024]{3,2,1,0:T(8,128)(2,1)} %get-tuple-element.49), kind=kLoop, calls=%fused_computation.4 | loop fusion | flops 1048576 | bytes 1572864 | tf_op jit(solution)/shard_map/convert_element_type | solution.py:105
  101.9 5.9 %all-to-all-done.refs_3_ = bf16[8,4,2,64,128]{4,3,2,1,0:T(8,128)(2,1)S(1)} async-done(((bf16[8,4,2,64,128]{4,3,2,1,0:T(8,128)(2,1)}), bf16[8,4,2,64,128]{4,3,2,1,0:T(8,128)(2,1)S(1)}, u32[]{:S(2)}, u32[]{:S(2)}) %all-to-all-start) | async-done | bytes 1048608 | tf_op jit(solution)/shard_map/all_to_all | solution.py:498
  107.9 5.2 %collective-permute-done.15 = bf16[2,1,128,1024]{3,2,1,0:T(8,128)(2,1)} collective-permute-done((bf16[2,1,128,1024]{3,2,1,0:T(8,128)(2,1)}, bf16[2,1,128,1024]{3,2,1,0:T(8,128)(2,1)}, u32[]{:S(2)}, u32[]{:S(2)}) %collective-permute-start.15) | collective-permute-done | bytes 524320 | tf_op jit(solution)/shard_map/ppermute | solution.py:76
  114.2 1.7 collective-permute-start.16
  115.9 7.0 %collective-permute-done.24 = bf16[1,2,128,1024]{3,2,1,0:T(8,128)(2,1)S(1)} collective-permute-done((bf16[1,2,128,1024]{3,2,1,0:T(8,128)(2,1)}, bf16[1,2,128,1024]{3,2,1,0:T(8,128)(2,1)S(1)}, u32[]{:S(2)}, u32[]{:S(2)}) %collective-permute-start.24) | collective-permute-done | bytes 524320 | tf_op jit(solution)/shard_map/ppermute | solution.py:76
  124.5 2.7 %collective-permute-done.16 = bf16[1,1,128,1024]{3,2,1,0:T(8,128)(2,1)S(1)} collective-permute-done((bf16[1,1,128,1024]{3,2,1,0:T(8,128)(2,1)S(1)}, bf16[1,1,128,1024]{3,2,1,0:T(8,128)(2,1)S(1)}, u32[]{:S(2)}, u32[]{:S(2)}) %collective-permute-start.16) | collective-permute-done | bytes 262176 | tf_op jit(solution)/shard_map/ppermute | solution.py:76
  128.5 1.5 collective-permute-start.18
  130.7 1.5 collective-permute-start.27
  132.8 5.0 %collective-permute-done.18.refs_7_.refs_8_ = bf16[128,1024]{1,0:T(8,128)(2,1)S(1)} collective-permute-done((bf16[128,1024]{1,0:T(8,128)(2,1)S(1)}, bf16[128,1024]{1,0:T(8,128)(2,1)S(1)}, u32[]{:S(2)}, u32[]{:S(2)}) %collective-permute-start.18) | collective-permute-done | bytes 262176 | tf_op jit(solution)/shard_map/ppermute | solution.py:59
  139.8 3.6 %collective-permute-done.27.refs_14_.refs_16_ = bf16[128,1024]{1,0:T(8,128)(2,1)S(1)} collective-permute-done((bf16[128,1024]{1,0:T(8,128)(2,1)S(1)}, bf16[128,1024]{1,0:T(8,128)(2,1)S(1)}, u32[]{:S(2)}, u32[]{:S(2)}) %collective-permute-start.27) | collective-permute-done | bytes 262176 | tf_op jit(solution)/shard_map/ppermute | solution.py:59
  145.4 3.6 %collective-permute-done.20.refs_9_.refs_10_ = bf16[128,1024]{1,0:T(8,128)(2,1)S(1)} collective-permute-done((bf16[128,1024]{1,0:T(8,128)(2,1)S(1)}, bf16[128,1024]{1,0:T(8,128)(2,1)S(1)}, u32[]{:S(2)}, u32[]{:S(2)}) %collective-permute-start.20) | collective-permute-done | bytes 262176 | tf_op jit(solution)/shard_map/ppermute | solution.py:59
  151.0 3.6 %collective-permute-done.29.refs_16_.refs_18_ = bf16[128,1024]{1,0:T(8,128)(2,1)S(1)} collective-permute-done((bf16[128,1024]{1,0:T(8,128)(2,1)S(1)}, bf16[128,1024]{1,0:T(8,128)(2,1)S(1)}, u32[]{:S(2)}, u32[]{:S(2)}) %collective-permute-start.29) | collective-permute-done | bytes 262176 | tf_op jit(solution)/shard_map/ppermute | solution.py:59
  156.6 3.6 %collective-permute-done.22.refs_11_.refs_12_ = bf16[128,1024]{1,0:T(8,128)(2,1)S(1)} collective-permute-done((bf16[128,1024]{1,0:T(8,128)(2,1)S(1)}, bf16[128,1024]{1,0:T(8,128)(2,1)S(1)}, u32[]{:S(2)}, u32[]{:S(2)}) %collective-permute-start.22) | collective-permute-done | bytes 262176 | tf_op jit(solution)/shard_map/ppermute | solution.py:59
  160.2 1.5 collective-permute-start.33
  162.4 3.5 %collective-permute-done.31.refs_18_.refs_20_ = bf16[128,1024]{1,0:T(8,128)(2,1)S(1)} collective-permute-done((bf16[128,1024]{1,0:T(8,128)(2,1)S(1)}, bf16[128,1024]{1,0:T(8,128)(2,1)S(1)}, u32[]{:S(2)}, u32[]{:S(2)}) %collective-permute-start.31) | collective-permute-done | bytes 262176 | tf_op jit(solution)/shard_map/ppermute | solution.py:59
  168.7 9.4 %attention.2 = (bf16[8,4,64,128]{3,2,1,0:T(8,128)(2,1)}, f32[2048,256]{1,0:T(8,128)}) custom-call(s32[2]{0:T(128)} %pad_add_fusion.refs_0_, s32[2,8]{1,0:T(2,128)} %constant.56.clone.refs_1_, s32[2]{0:T(128)} %refs_2_.5, bf16[8,4,2,64,128]{4,3,2,1,0:T(8,128)(2,1)} %copy-done, bf16[2048,256]{1,0:T(8,128)(2,1)} %bitcast.40, bf16[128,1024]{1,0:T(8,128)(2,1)} %copy-done.26, ...), custom_call_target="tpu_custom_call" | custom-call | tf_op jit(solution)/shard_map/attention/pallas_call | solution.py:444
  178.9 10.1 %attention.3 = (bf16[8,4,2,64,128]{4,3,2,1,0:T(8,128)(2,1)}, bf16[4096,128]{1,0:T(8,128)(2,1)}) custom-call(s32[2]{0:T(128)} %pad_add_fusion.refs_0_, s32[2,8]{1,0:T(2,128)} %constant.56.clone.refs_1_, s32[2]{0:T(128)} %refs_2_.5, bf16[8,4,2,64,128]{4,3,2,1,0:T(8,128)(2,1)} %copy-done, bf16[2048,256]{1,0:T(8,128)(2,1)} %bitcast.41, ...), custom_call_target="tpu_custom_call" | custom-call | tf_op jit(solution)/shard_map/attention/pallas_call | solution.py:444
  190.5 4.0 %all-to-all-start.1 = ((bf16[8,4,2,64,128]{4,3,2,1,0:T(8,128)(2,1)}), bf16[8,4,2,64,128]{4,3,2,1,0:T(8,128)(2,1)S(1)}, u32[]{:S(2)}, u32[]{:S(2)}) async-start(bf16[8,4,2,64,128]{4,3,2,1,0:T(8,128)(2,1)} %get-tuple-element.57), calls=%async_computation.1 | async-start | bytes 2097152 | tf_op jit(solution)/shard_map/all_to_all | solution.py:512
  194.5 15.2 %collective-permute-done.36 = bf16[4096,128]{1,0:T(8,128)(2,1)} collective-permute-done((bf16[4096,128]{1,0:T(8,128)(2,1)}, bf16[4096,128]{1,0:T(8,128)(2,1)}, u32[]{:S(2)}, u32[]{:S(2)}) %collective-permute-start.36) | collective-permute-done | bytes 1048608 | tf_op jit(solution)/shard_map/ppermute | solution.py:76
  211.2 5.1 %all-to-all-done.1.packed = bf16[8,4,2,64,128]{4,3,2,1,0:T(8,128)(2,1)S(1)} async-done(((bf16[8,4,2,64,128]{4,3,2,1,0:T(8,128)(2,1)}), bf16[8,4,2,64,128]{4,3,2,1,0:T(8,128)(2,1)S(1)}, u32[]{:S(2)}, u32[]{:S(2)}) %all-to-all-start.1) | async-done | bytes 1048608 | tf_op jit(solution)/shard_map/all_to_all | solution.py:512
  217.3 2.5 %unpack.1 = (bf16[2,64,1024]{2,1,0:T(8,128)(2,1)}, bf16[3,2,64,1024]{3,2,1,0:T(8,128)(2,1)}) custom-call(bf16[8,4,2,64,128]{4,3,2,1,0:T(8,128)(2,1)} %copy-done.3), custom_call_target="tpu_custom_call" | custom-call | tf_op jit(solution)/shard_map/unpack/pallas_call | solution.py:199
  (160 shorter events, 43.5 us)
Async XLA Ops:
  3.1 29.6 %collective-permute-start.1 = (bf16[1056,256]{1,0:T(8,128)(2,1)S(1)}, bf16[1056,256]{1,0:T(8,128)(2,1)S(1)}, u32[]{:S(2)}, u32[]{:S(2)}) collective-permute-start(bf16[1056,256]{1,0:T(8,128)(2,1)S(1)} %pad_maximum_fusion.2.refs_5_.refs_9_), channel_id=1, source_target_pairs={{0,4},{1,5},{2,6},{3,7},{4,0},{5,1},{6,2},{7,3},{8,12},{9,13},{10,... | collective-permute-start | bytes 1622024 | tf_op jit(solution)/shard_map/ppermute | solution.py:76
  7.2 25.5 %collective-permute-start = (bf16[1056,256]{1,0:T(8,128)(2,1)S(1)}, bf16[1056,256]{1,0:T(8,128)(2,1)S(1)}, u32[]{:S(2)}, u32[]{:S(2)}) collective-permute-start(bf16[1056,256]{1,0:T(8,128)(2,1)S(1)} %pad_maximum_fusion.2.refs_5_.refs_9_), channel_id=1, source_target_pairs={{0,1},{1,0},{2,3},{3,2},{4,5},{5,4},{6,7},{7,6},{8,9},{9,8},{10,11... | collective-permute-start | bytes 1622024 | tf_op jit(solution)/shard_map/ppermute | solution.py:76
  8.7 23.9 %collective-permute-start.2 = (bf16[1056,256]{1,0:T(8,128)(2,1)S(1)}, bf16[1056,256]{1,0:T(8,128)(2,1)S(1)}, u32[]{:S(2)}, u32[]{:S(2)}) collective-permute-start(bf16[1056,256]{1,0:T(8,128)(2,1)S(1)} %pad_maximum_fusion.1), channel_id=1, source_target_pairs={{0,2},{1,3},{2,0},{3,1},{4,6},{5,7},{6,4},{7,5},{8,10},{9,11},{10,... | collective-permute-start | bytes 1622024 | tf_op jit(solution)/shard_map/ppermute | solution.py:76
  32.7 28.8 %collective-permute-start.3 = (bf16[144,2048]{1,0:T(8,128)(2,1)S(1)}, bf16[144,2048]{1,0:T(8,128)(2,1)}, u32[]{:S(2)}, u32[]{:S(2)}) collective-permute-start(bf16[144,2048]{1,0:T(8,128)(2,1)S(1)} %pad_maximum_fusion.refs_1_), channel_id=1, source_target_pairs={{0,2},{1,3},{2,0},{3,1},{4,6},{5,7},{6,4},{7,5},{8,10},{9,11},{10,... | collective-permute-start | bytes 1769480 | tf_op jit(solution)/shard_map/ppermute | solution.py:76
  32.9 28.6 %collective-permute-start.4 = (bf16[144,2048]{1,0:T(8,128)(2,1)S(1)}, bf16[144,2048]{1,0:T(8,128)(2,1)S(1)}, u32[]{:S(2)}, u32[]{:S(2)}) collective-permute-start(bf16[144,2048]{1,0:T(8,128)(2,1)S(1)} %pad_maximum_fusion.refs_1_), channel_id=1, source_target_pairs={{0,16},{8,24},{16,0},{24,8},{1,17},{9,25},{17,1},{25,9},{2,18},{10... | collective-permute-start | bytes 1769480 | tf_op jit(solution)/shard_map/ppermute | solution.py:76
  34.4 25.6 %collective-permute-start.5 = (bf16[1056,256]{1,0:T(8,128)(2,1)S(1)}, bf16[1056,256]{1,0:T(8,128)(2,1)}, u32[]{:S(2)}, u32[]{:S(2)}) collective-permute-start(bf16[1056,256]{1,0:T(8,128)(2,1)S(1)} %pad_maximum_fusion.1), channel_id=1, source_target_pairs={{0,6},{1,7},{2,4},{3,5},{4,2},{5,3},{6,0},{7,1},{8,14},{9,15},{10,... | collective-permute-start | bytes 1622024 | tf_op jit(solution)/shard_map/ppermute | solution.py:76
  36.8 23.2 %collective-permute-start.6 = (bf16[1056,256]{1,0:T(8,128)(2,1)S(1)}, bf16[1056,256]{1,0:T(8,128)(2,1)S(1)}, u32[]{:S(2)}, u32[]{:S(2)}) collective-permute-start(bf16[1056,256]{1,0:T(8,128)(2,1)S(1)} %collective-permute-done.1.refs_9_.refs_13_), channel_id=1, source_target_pairs={{0,1},{1,0},{2,3},{3,2},{4,5},{5,4},{6,7},{7,6},{8,9},{9,8},{10,11... | collective-permute-start | bytes 1622024 | tf_op jit(solution)/shard_map/ppermute | solution.py:76
  37.7 23.7 %collective-permute-start.7 = (bf16[1056,256]{1,0:T(8,128)(2,1)S(1)}, bf16[1056,256]{1,0:T(8,128)(2,1)S(1)}, u32[]{:S(2)}, u32[]{:S(2)}) collective-permute-start(bf16[1056,256]{1,0:T(8,128)(2,1)S(1)} %collective-permute-done.2.refs_7_.refs_11_), channel_id=1, source_target_pairs={{0,1},{1,0},{2,3},{3,2},{4,5},{5,4},{6,7},{7,6},{8,9},{9,8},{10,11... | collective-permute-start | bytes 1622024 | tf_op jit(solution)/shard_map/ppermute | solution.py:76
  61.6 16.1 %collective-permute-start.9 = (bf16[144,2048]{1,0:T(8,128)(2,1)}, bf16[144,2048]{1,0:T(8,128)(2,1)}, u32[]{:S(2)}, u32[]{:S(2)}) collective-permute-start(bf16[144,2048]{1,0:T(8,128)(2,1)} %collective-permute-done.3.refs_5_), channel_id=1, source_target_pairs={{0,16},{8,24},{16,0},{24,8},{1,17},{9,25},{17,1},{25,9},{2,18},{10... | collective-permute-start | bytes 1769480 | tf_op jit(solution)/shard_map/ppermute | solution.py:76
  62.3 14.6 %collective-permute-start.8 = (bf16[1056,256]{1,0:T(8,128)(2,1)}, bf16[1056,256]{1,0:T(8,128)(2,1)S(1)}, u32[]{:S(2)}, u32[]{:S(2)}) collective-permute-start(bf16[1056,256]{1,0:T(8,128)(2,1)} %collective-permute-done.5.refs_15_), channel_id=1, source_target_pairs={{0,1},{1,0},{2,3},{3,2},{4,5},{5,4},{6,7},{7,6},{8,9},{9,8},{10,11... | collective-permute-start | bytes 1622024 | tf_op jit(solution)/shard_map/ppermute | solution.py:76
  64.3 16.9 %collective-permute-start.12 = (bf16[144,2048]{1,0:T(8,128)(2,1)}, bf16[144,2048]{1,0:T(8,128)(2,1)}, u32[]{:S(2)}, u32[]{:S(2)}) collective-permute-start(bf16[144,2048]{1,0:T(8,128)(2,1)} %collective-permute-done.3.refs_5_), channel_id=1, source_target_pairs={{0,8},{8,0},{16,24},{24,16},{1,9},{9,1},{17,25},{25,17},{2,10},{10... | collective-permute-start | bytes 1769480 | tf_op jit(solution)/shard_map/ppermute | solution.py:76
  77.6 30.2 %all-to-all-start = ((bf16[8,4,2,64,128]{4,3,2,1,0:T(8,128)(2,1)}), bf16[8,4,2,64,128]{4,3,2,1,0:T(8,128)(2,1)S(1)}, u32[]{:S(2)}, u32[]{:S(2)}) async-start(bf16[8,4,2,64,128]{4,3,2,1,0:T(8,128)(2,1)} %pack.1), calls=%async_computation | async-start | bytes 2097152 | tf_op jit(solution)/shard_map/all_to_all | solution.py:498
  98.5 14.5 %collective-permute-start.15 = (bf16[2,1,128,1024]{3,2,1,0:T(8,128)(2,1)}, bf16[2,1,128,1024]{3,2,1,0:T(8,128)(2,1)}, u32[]{:S(2)}, u32[]{:S(2)}) collective-permute-start(bf16[2,1,128,1024]{3,2,1,0:T(8,128)(2,1)} %add_convert_fusion.2), channel_id=1, source_target_pairs={{0,16},{8,24},{16,0},{24,8},{1,17},{9,25},{17,1},{25,9},{2,18},{10... | collective-permute-start | bytes 1572872 | tf_op jit(solution)/shard_map/ppermute | solution.py:76
  107.9 15.0 %collective-permute-start.24 = (bf16[1,2,128,1024]{3,2,1,0:T(8,128)(2,1)}, bf16[1,2,128,1024]{3,2,1,0:T(8,128)(2,1)S(1)}, u32[]{:S(2)}, u32[]{:S(2)}) collective-permute-start(bf16[1,2,128,1024]{3,2,1,0:T(8,128)(2,1)} %add_convert_fusion.1), channel_id=1, source_target_pairs={{0,2},{1,3},{2,0},{3,1},{4,6},{5,7},{6,4},{7,5},{8,10},{9,11},{10,... | collective-permute-start | bytes 1572872 | tf_op jit(solution)/shard_map/ppermute | solution.py:76
  114.2 13.1 %collective-permute-start.16 = (bf16[1,1,128,1024]{3,2,1,0:T(8,128)(2,1)S(1)}, bf16[1,1,128,1024]{3,2,1,0:T(8,128)(2,1)S(1)}, u32[]{:S(2)}, u32[]{:S(2)}) collective-permute-start(bf16[1,1,128,1024]{3,2,1,0:T(8,128)(2,1)S(1)} %add_convert_fusion.6), channel_id=1, source_target_pairs={{0,2},{1,3},{2,0},{3,1},{4,6},{5,7},{6,4},{7,5},{8,10},{9,11},{10,... | collective-permute-start | bytes 786440 | tf_op jit(solution)/shard_map/ppermute | solution.py:76
  128.5 9.3 %collective-permute-start.18 = (bf16[128,1024]{1,0:T(8,128)(2,1)S(1)}, bf16[128,1024]{1,0:T(8,128)(2,1)S(1)}, u32[]{:S(2)}, u32[]{:S(2)}) collective-permute-start(bf16[128,1024]{1,0:T(8,128)(2,1)S(1)} %fusion.refs_5_), channel_id=1, source_target_pairs={{0,1},{2,0},{4,2},{6,4},{7,6},{5,7},{3,5},{1,3},{8,9},{10,8},{12,1... | collective-permute-start | bytes 786440 | tf_op jit(solution)/shard_map/ppermute | solution.py:59
  130.7 12.6 %collective-permute-start.27 = (bf16[128,1024]{1,0:T(8,128)(2,1)S(1)}, bf16[128,1024]{1,0:T(8,128)(2,1)S(1)}, u32[]{:S(2)}, u32[]{:S(2)}) collective-permute-start(bf16[128,1024]{1,0:T(8,128)(2,1)S(1)} %fusion.1.refs_12_), channel_id=1, source_target_pairs={{0,1},{2,0},{4,2},{6,4},{7,6},{5,7},{3,5},{1,3},{8,9},{10,8},{12,1... | collective-permute-start | bytes 786440 | tf_op jit(solution)/shard_map/ppermute | solution.py:59
  132.3 12.6 %collective-permute-start.26 = (bf16[128,1024]{1,0:T(8,128)(2,1)S(1)}, bf16[128,1024]{1,0:T(8,128)(2,1)S(1)}, u32[]{:S(2)}, u32[]{:S(2)}) collective-permute-start(bf16[128,1024]{1,0:T(8,128)(2,1)S(1)} %fusion.1.refs_12_), channel_id=1, source_target_pairs={{0,2},{2,4},{4,6},{6,7},{7,5},{5,3},{3,1},{1,0},{8,10},{10,12},{12... | collective-permute-start | bytes 786440 | tf_op jit(solution)/shard_map/ppermute | solution.py:58
  137.8 11.2 %collective-permute-start.20 = (bf16[128,1024]{1,0:T(8,128)(2,1)S(1)}, bf16[128,1024]{1,0:T(8,128)(2,1)S(1)}, u32[]{:S(2)}, u32[]{:S(2)}) collective-permute-start(bf16[128,1024]{1,0:T(8,128)(2,1)S(1)} %collective-permute-done.18.refs_7_.refs_8_), channel_id=1, source_target_pairs={{0,1},{2,0},{4,2},{6,4},{7,6},{5,7},{3,5},{1,3},{8,9},{10,8},{12,1... | collective-permute-start | bytes 786440 | tf_op jit(solution)/shard_map/ppermute | solution.py:59
  139.2 11.2 %collective-permute-start.19 = (bf16[128,1024]{1,0:T(8,128)(2,1)S(1)}, bf16[128,1024]{1,0:T(8,128)(2,1)S(1)}, u32[]{:S(2)}, u32[]{:S(2)}) collective-permute-start(bf16[128,1024]{1,0:T(8,128)(2,1)S(1)} %collective-permute-done.17.refs_6_.refs_7_), channel_id=1, source_target_pairs={{0,2},{2,4},{4,6},{6,7},{7,5},{5,3},{3,1},{1,0},{8,10},{10,12},{12... | collective-permute-start | bytes 786440 | tf_op jit(solution)/shard_map/ppermute | solution.py:58
  143.4 11.2 %collective-permute-start.29 = (bf16[128,1024]{1,0:T(8,128)(2,1)S(1)}, bf16[128,1024]{1,0:T(8,128)(2,1)S(1)}, u32[]{:S(2)}, u32[]{:S(2)}) collective-permute-start(bf16[128,1024]{1,0:T(8,128)(2,1)S(1)} %collective-permute-done.27.refs_14_.refs_16_), channel_id=1, source_target_pairs={{0,1},{2,0},{4,2},{6,4},{7,6},{5,7},{3,5},{1,3},{8,9},{10,8},{12,1... | collective-permute-start | bytes 786440 | tf_op jit(solution)/shard_map/ppermute | solution.py:59
  144.9 11.2 %collective-permute-start.28 = (bf16[128,1024]{1,0:T(8,128)(2,1)S(1)}, bf16[128,1024]{1,0:T(8,128)(2,1)S(1)}, u32[]{:S(2)}, u32[]{:S(2)}) collective-permute-start(bf16[128,1024]{1,0:T(8,128)(2,1)S(1)} %collective-permute-done.26.refs_13_.refs_15_), channel_id=1, source_target_pairs={{0,2},{2,4},{4,6},{6,7},{7,5},{5,3},{3,1},{1,0},{8,10},{10,12},{12... | collective-permute-start | bytes 786440 | tf_op jit(solution)/shard_map/ppermute | solution.py:58
  149.0 11.2 %collective-permute-start.22 = (bf16[128,1024]{1,0:T(8,128)(2,1)S(1)}, bf16[128,1024]{1,0:T(8,128)(2,1)S(1)}, u32[]{:S(2)}, u32[]{:S(2)}) collective-permute-start(bf16[128,1024]{1,0:T(8,128)(2,1)S(1)} %collective-permute-done.20.refs_9_.refs_10_), channel_id=1, source_target_pairs={{0,1},{2,0},{4,2},{6,4},{7,6},{5,7},{3,5},{1,3},{8,9},{10,8},{12,1... | collective-permute-start | bytes 786440 | tf_op jit(solution)/shard_map/ppermute | solution.py:59
  150.5 11.3 %collective-permute-start.21 = (bf16[128,1024]{1,0:T(8,128)(2,1)S(1)}, bf16[128,1024]{1,0:T(8,128)(2,1)S(1)}, u32[]{:S(2)}, u32[]{:S(2)}) collective-permute-start(bf16[128,1024]{1,0:T(8,128)(2,1)S(1)} %collective-permute-done.19.refs_8_.refs_9_), channel_id=1, source_target_pairs={{0,2},{2,4},{4,6},{6,7},{7,5},{5,3},{3,1},{1,0},{8,10},{10,12},{12... | collective-permute-start | bytes 786440 | tf_op jit(solution)/shard_map/ppermute | solution.py:58
  154.6 11.2 %collective-permute-start.31 = (bf16[128,1024]{1,0:T(8,128)(2,1)S(1)}, bf16[128,1024]{1,0:T(8,128)(2,1)S(1)}, u32[]{:S(2)}, u32[]{:S(2)}) collective-permute-start(bf16[128,1024]{1,0:T(8,128)(2,1)S(1)} %collective-permute-done.29.refs_16_.refs_18_), channel_id=1, source_target_pairs={{0,1},{2,0},{4,2},{6,4},{7,6},{5,7},{3,5},{1,3},{8,9},{10,8},{12,1... | collective-permute-start | bytes 786440 | tf_op jit(solution)/shard_map/ppermute | solution.py:59
  156.1 11.3 %collective-permute-start.30 = (bf16[128,1024]{1,0:T(8,128)(2,1)S(1)}, bf16[128,1024]{1,0:T(8,128)(2,1)S(1)}, u32[]{:S(2)}, u32[]{:S(2)}) collective-permute-start(bf16[128,1024]{1,0:T(8,128)(2,1)S(1)} %collective-permute-done.28.refs_15_.refs_17_), channel_id=1, source_target_pairs={{0,2},{2,4},{4,6},{6,7},{7,5},{5,3},{3,1},{1,0},{8,10},{10,12},{12... | collective-permute-start | bytes 786440 | tf_op jit(solution)/shard_map/ppermute | solution.py:58
  160.2 17.9 %collective-permute-start.33 = (bf16[64,1024]{1,0:T(8,128)(2,1)S(1)}, bf16[64,1024]{1,0:T(8,128)(2,1)S(1)}, u32[]{:S(2)}, u32[]{:S(2)}) collective-permute-start(bf16[64,1024]{1,0:T(8,128)(2,1)S(1)} %slice.113), channel_id=1, source_target_pairs={{0,1},{2,0},{4,2},{6,4},{7,6},{5,7},{3,5},{1,3},{8,9},{10,8},{12,1... | collective-permute-start | bytes 393224 | tf_op jit(solution)/shard_map/ppermute | solution.py:63
  161.8 16.4 %collective-permute-start.32 = (bf16[64,1024]{1,0:T(8,128)(2,1)S(1)}, bf16[64,1024]{1,0:T(8,128)(2,1)S(1)}, u32[]{:S(2)}, u32[]{:S(2)}) collective-permute-start(bf16[64,1024]{1,0:T(8,128)(2,1)S(1)} %slice.112), channel_id=1, source_target_pairs={{0,2},{2,4},{4,6},{6,7},{7,5},{5,3},{3,1},{1,0},{8,10},{10,12},{12... | collective-permute-start | bytes 393224 | tf_op jit(solution)/shard_map/ppermute | solution.py:62
  165.9 12.3 %collective-permute-start.35 = (bf16[64,1024]{1,0:T(8,128)(2,1)S(1)}, bf16[64,1024]{1,0:T(8,128)(2,1)S(1)}, u32[]{:S(2)}, u32[]{:S(2)}) collective-permute-start(bf16[64,1024]{1,0:T(8,128)(2,1)S(1)} %slice.115), channel_id=1, source_target_pairs={{0,1},{2,0},{4,2},{6,4},{7,6},{5,7},{3,5},{1,3},{8,9},{10,8},{12,1... | collective-permute-start | bytes 393224 | tf_op jit(solution)/shard_map/ppermute | solution.py:63
  168.1 10.1 %collective-permute-start.34 = (bf16[64,1024]{1,0:T(8,128)(2,1)}, bf16[64,1024]{1,0:T(8,128)(2,1)S(1)}, u32[]{:S(2)}, u32[]{:S(2)}) collective-permute-start(bf16[64,1024]{1,0:T(8,128)(2,1)} %slice.114), channel_id=1, source_target_pairs={{0,2},{2,4},{4,6},{6,7},{7,5},{5,3},{3,1},{1,0},{8,10},{10,12},{12... | collective-permute-start | bytes 393224 | tf_op jit(solution)/shard_map/ppermute | solution.py:62
  189.0 20.6 %collective-permute-start.36 = (bf16[4096,128]{1,0:T(8,128)(2,1)}, bf16[4096,128]{1,0:T(8,128)(2,1)}, u32[]{:S(2)}, u32[]{:S(2)}) collective-permute-start(bf16[4096,128]{1,0:T(8,128)(2,1)} %get-tuple-element.60), channel_id=1, source_target_pairs={{0,16},{8,24},{16,0},{24,8},{1,17},{9,25},{17,1},{25,9},{2,18},{10... | collective-permute-start | bytes 3145736 | tf_op jit(solution)/shard_map/ppermute | solution.py:76
  190.5 25.8 %all-to-all-start.1 = ((bf16[8,4,2,64,128]{4,3,2,1,0:T(8,128)(2,1)}), bf16[8,4,2,64,128]{4,3,2,1,0:T(8,128)(2,1)S(1)}, u32[]{:S(2)}, u32[]{:S(2)}) async-start(bf16[8,4,2,64,128]{4,3,2,1,0:T(8,128)(2,1)} %get-tuple-element.57), calls=%async_computation.1 | async-start | bytes 2097152 | tf_op jit(solution)/shard_map/all_to_all | solution.py:512
  (50 other events, 584.0 us)

commit v2 on v0

--- a/solution.py
+++ b/solution.py
@@ -90,23 +90,26 @@
 def reduce_rows(keep, send, pair_first, after):
     langs = lax.axis_size("lang")
 
-    def over_pair(parts):
-        kept, sent = parts
-        arrived = xor_swap(tie(sent.astype(BF16), after), "seq", PAIR)
-        return kept + arrived.astype(F32)
-
-    arrived = xor_swap(send, "lang", 1)
-    halves = [keep[side].astype(F32) + arrived[side].astype(F32) for side in range(2)]
+    def total(terms):
+        return functools.reduce(lambda a, b: a + b, [term.astype(F32) for term in terms])
+
+    def over_pair(terms):
+        sent = total([term[1:] for term in terms]).astype(BF16)
+        return [term[:1] for term in terms] + [xor_swap(sent, "seq", PAIR)]
+
+    terms = [keep, xor_swap(send, "lang", 1)]
     if pair_first:
-        halves = [over_pair(halves)]
+        terms = over_pair(terms)
     mask = 2
     while mask < langs:
-        sent = jnp.stack([half[1::2] for half in halves]).astype(BF16)
-        arrived = xor_swap(sent, "lang", mask).astype(F32)
-        halves = [half[0::2] + arrived[side] for side, half in enumerate(halves)]
+        sent = total([term[:, 1::2] for term in terms]).astype(BF16)
+        if not pair_first and mask == 2:
+            sent = tie(sent, after)
+        terms = [term[:, 0::2] for term in terms] + [xor_swap(sent, "lang", mask)]
         mask *= 2
-    total = halves[0] if pair_first else over_pair(halves)
-    return total[0].astype(BF16)
+    if not pair_first:
+        terms = over_pair(terms)
+    return total(terms)[0, 0].astype(BF16)
 
 
 def split_halves(block, seq_index):

time: 218 us -> 221 us (1.014)
    convert_element_type x5 -> x6, other arithmetic: 2.36 us -> 6.08 us  [the longest x2 2.57 us: over_pair(): sent = total([term[1:] for term in terms]).astype(BF16)]
    unnamed x81 -> x85, local copies, waits for them, and re-layouts: 6.49 us -> 7.1 us
where the time goes in v2:
time: 221 us
  waiting for transfers between devices  118 us (53%)
  starting transfers between devices  47.9 us (22%)
  Pallas kernels  34 us (15%)
  other arithmetic  9.83 us (4%)
  local copies, waits for them, and re-layouts  9.42 us (4%)
    ppermute x22, waiting for transfers between devices, xor_swap(): return lax.ppermute(array, axis, [(i, i ^ mask) for i in range(count)])  79.7 us
    ppermute x6, waiting for transfers between devices, ring_gather(): down = lax.ppermute(down, 'seq', back)  22.7 us
    ppermute x22, starting transfers between devices, xor_swap(): return lax.ppermute(array, axis, [(i, i ^ mask) for i in range(count)])  22.6 us
    pallas_call x1, Pallas kernels, attention_stage(): pl.pallas_call(body, out_shape=(jax.ShapeDtypeStruct(latents.shape, BF16)...  13.1 us
    pallas_call x1, Pallas kernels, expert_stage(): pl.pallas_call(body, out_shape=(shape,) * 4, in_specs=[smem()] + [vmem()]...  10.9 us
    ppermute x6, starting transfers between devices, ring_gather(): down = lax.ppermute(down, 'seq', back)  8.95 us
    unnamed x85, local copies, waits for them, and re-layouts  7.1 us
    all_to_all x1, waiting for transfers between devices, local(): lax.all_to_all(out, 'seq', split_axis=0, concat_axis=0, tiled=True)  5.76 us
  transfers between devices with their start and end apart: 40, of which 21 were waited for; matrix products, arithmetic and copies ran while one was open for 4% of the time, Pallas kernels for 10%

profile of v2, /device:TPU:0, one launch (start us, length us, event | category | flops | bytes accessed | tf_op | source)
XLA Modules:
  0.0 220.5 jit_solution(5878097938259660939)
XLA Ops:
  3.1 4.1 %collective-permute-start.1 = (bf16[1056,256]{1,0:T(8,128)(2,1)S(1)}, bf16[1056,256]{1,0:T(8,128)(2,1)S(1)}, u32[]{:S(2)}, u32[]{:S(2)}) collective-permute-start(bf16[1056,256]{1,0:T(8,128)(2,1)S(1)} %pad_maximum_fusion.2.refs_5_.refs_9_), channel_id=1, source_target_pairs={{0,4},{1,5},{2,6},{3,7},{4,0},{5,1},{6,2},{7,3},{8,12},{9,13},{10,... | collective-permute-start | bytes 1622024 | tf_op jit(solution)/shard_map/ppermute | solution.py:76
  8.7 1.6 collective-permute-start.2
  11.5 2.4 %pack.1 = bf16[8,4,2,64,128]{4,3,2,1,0:T(8,128)(2,1)} custom-call(bf16[2,64,1024]{2,1,0:T(8,128)(2,1)} %refs_0_.1, bf16[2,64,1024]{2,1,0:T(8,128)(2,1)} %refs_1_.2, bf16[2,64,1024]{2,1,0:T(8,128)(2,1)} %refs_2_.2, bf16[2,64,1024]{2,1,0:T(8,128)(2,1)} %refs_3_.1), custom_call_target="tpu_custom_call" | custom-call | tf_op jit(solution)/shard_map/pack/pallas_call | solution.py:181
  14.0 18.7 %collective-permute-done.2.refs_7_.refs_11_ = bf16[1056,256]{1,0:T(8,128)(2,1)S(1)} collective-permute-done((bf16[1056,256]{1,0:T(8,128)(2,1)S(1)}, bf16[1056,256]{1,0:T(8,128)(2,1)S(1)}, u32[]{:S(2)}, u32[]{:S(2)}) %collective-permute-start.2) | collective-permute-done | bytes 540704 | tf_op jit(solution)/shard_map/ppermute | solution.py:76
  34.4 2.4 %collective-permute-start.5 = (bf16[1056,256]{1,0:T(8,128)(2,1)S(1)}, bf16[1056,256]{1,0:T(8,128)(2,1)}, u32[]{:S(2)}, u32[]{:S(2)}) collective-permute-start(bf16[1056,256]{1,0:T(8,128)(2,1)S(1)} %pad_maximum_fusion.1), channel_id=1, source_target_pairs={{0,6},{1,7},{2,4},{3,5},{4,2},{5,3},{6,0},{7,1},{8,14},{9,15},{10,... | collective-permute-start | bytes 1622024 | tf_op jit(solution)/shard_map/ppermute | solution.py:76
  38.8 21.1 %collective-permute-done.5.refs_15_ = bf16[1056,256]{1,0:T(8,128)(2,1)} collective-permute-done((bf16[1056,256]{1,0:T(8,128)(2,1)S(1)}, bf16[1056,256]{1,0:T(8,128)(2,1)}, u32[]{:S(2)}, u32[]{:S(2)}) %collective-permute-start.5) | collective-permute-done | bytes 540704 | tf_op jit(solution)/shard_map/ppermute | solution.py:76
  66.0 5.1 %hidden_sums.1.refs_17_ = f32[512,704]{1,0:T(8,128)} custom-call(s32[2]{0:T(128)} %pad_add_fusion.refs_0_, bf16[144,2048]{1,0:T(8,128)(2,1)} %copy-done, bf16[144,2048]{1,0:T(8,128)(2,1)} %copy-done.5, bf16[144,2048]{1,0:T(8,128)(2,1)} %copy-done.4, bf16[144,2048]{1,0:T(8,128)(2,1)} %copy-done.6, bf16[1056,256]{1,0:T(8,128)(2,1)} %copy-done.1, ...), custom_call_target="tpu_custom_call" | custom-call | tf_op jit(solution)/shard_map/hidden_sums/pallas_call | solution.py:257
  71.1 5.7 %collective-permute-done.8.refs_16_ = bf16[1056,256]{1,0:T(8,128)(2,1)S(1)} collective-permute-done((bf16[1056,256]{1,0:T(8,128)(2,1)}, bf16[1056,256]{1,0:T(8,128)(2,1)S(1)}, u32[]{:S(2)}, u32[]{:S(2)}) %collective-permute-start.8) | collective-permute-done | bytes 540704 | tf_op jit(solution)/shard_map/ppermute | solution.py:76
  77.6 3.6 %all-to-all-start = ((bf16[8,4,2,64,128]{4,3,2,1,0:T(8,128)(2,1)}), bf16[8,4,2,64,128]{4,3,2,1,0:T(8,128)(2,1)S(1)}, u32[]{:S(2)}, u32[]{:S(2)}) async-start(bf16[8,4,2,64,128]{4,3,2,1,0:T(8,128)(2,1)} %pack.1), calls=%async_computation | async-start | bytes 2097152 | tf_op jit(solution)/shard_map/all_to_all | solution.py:479
  82.0 10.9 %expert.1 = (bf16[2,2,128,1024]{3,2,1,0:T(8,128)(2,1)}, bf16[2,2,128,1024]{3,2,1,0:T(8,128)(2,1)}, bf16[2,2,128,1024]{3,2,1,0:T(8,128)(2,1)}, bf16[2,2,128,1024]{3,2,1,0:T(8,128)(2,1)}) custom-call(s32[2]{0:T(128)} %pad_add_fusion.refs_0_, bf16[144,2048]{1,0:T(8,128)(2,1)} %copy-done, bf16[144,2048]{1,0:T(8,128)(2,1)} %copy-done.5, ...), custom_call_target="tpu_custom_call" | custom-call | tf_op jit(solution)/shard_map/expert/pallas_call | solution.py:318
  93.6 2.4 %collective-permute-done.25 = bf16[2,2,128,1024]{3,2,1,0:T(8,128)(2,1)S(1)} collective-permute-done((bf16[2,2,128,1024]{3,2,1,0:T(8,128)(2,1)}, bf16[2,2,128,1024]{3,2,1,0:T(8,128)(2,1)S(1)}, u32[]{:S(2)}, u32[]{:S(2)}) %collective-permute-start.25) | collective-permute-done | bytes 1048608 | tf_op jit(solution)/shard_map/ppermute | solution.py:76
  96.0 2.4 %add_convert_fusion.1 = bf16[1,2,128,1024]{3,2,1,0:T(8,128)(2,1)} fusion(bf16[2,2,128,1024]{3,2,1,0:T(8,128)(2,1)S(1)} %collective-permute-done.25, bf16[2,2,128,1024]{3,2,1,0:T(8,128)(2,1)} %get-tuple-element.49), kind=kLoop, calls=%fused_computation.3 | loop fusion | flops 1048576 | bytes 1572864 | tf_op jit(solution)/shard_map/convert_element_type | solution.py:97
  98.5 1.8 collective-permute-start.26
  102.3 5.7 %all-to-all-done.refs_3_ = bf16[8,4,2,64,128]{4,3,2,1,0:T(8,128)(2,1)S(1)} async-done(((bf16[8,4,2,64,128]{4,3,2,1,0:T(8,128)(2,1)}), bf16[8,4,2,64,128]{4,3,2,1,0:T(8,128)(2,1)S(1)}, u32[]{:S(2)}, u32[]{:S(2)}) %all-to-all-start) | async-done | bytes 1048608 | tf_op jit(solution)/shard_map/all_to_all | solution.py:479
  109.4 8.2 %collective-permute-done.26 = bf16[1,2,128,1024]{3,2,1,0:T(8,128)(2,1)} collective-permute-done((bf16[1,2,128,1024]{3,2,1,0:T(8,128)(2,1)}, bf16[1,2,128,1024]{3,2,1,0:T(8,128)(2,1)}, u32[]{:S(2)}, u32[]{:S(2)}) %collective-permute-start.26) | collective-permute-done | bytes 524320 | tf_op jit(solution)/shard_map/ppermute | solution.py:76
  120.2 2.2 collective-permute-done.15
  122.7 4.6 %collective-permute-done.27 = bf16[1,1,128,1024]{3,2,1,0:T(8,128)(2,1)S(1)} collective-permute-done((bf16[1,1,128,1024]{3,2,1,0:T(8,128)(2,1)S(1)}, bf16[1,1,128,1024]{3,2,1,0:T(8,128)(2,1)S(1)}, u32[]{:S(2)}, u32[]{:S(2)}) %collective-permute-start.27) | collective-permute-done | bytes 262176 | tf_op jit(solution)/shard_map/ppermute | solution.py:76
  128.5 1.5 collective-permute-start.29
  130.8 1.5 collective-permute-start.18
  132.9 4.9 %collective-permute-done.29.refs_16_ = bf16[128,1024]{1,0:T(8,128)(2,1)S(1)} collective-permute-done((bf16[128,1024]{1,0:T(8,128)(2,1)S(1)}, bf16[128,1024]{1,0:T(8,128)(2,1)S(1)}, u32[]{:S(2)}, u32[]{:S(2)}) %collective-permute-start.29) | collective-permute-done | bytes 262176 | tf_op jit(solution)/shard_map/ppermute | solution.py:59
  139.8 3.6 %collective-permute-done.18.refs_7_ = bf16[128,1024]{1,0:T(8,128)(2,1)S(1)} collective-permute-done((bf16[128,1024]{1,0:T(8,128)(2,1)S(1)}, bf16[128,1024]{1,0:T(8,128)(2,1)S(1)}, u32[]{:S(2)}, u32[]{:S(2)}) %collective-permute-start.18) | collective-permute-done | bytes 262176 | tf_op jit(solution)/shard_map/ppermute | solution.py:59
  145.5 3.6 %collective-permute-done.31.refs_18_ = bf16[128,1024]{1,0:T(8,128)(2,1)S(1)} collective-permute-done((bf16[128,1024]{1,0:T(8,128)(2,1)S(1)}, bf16[128,1024]{1,0:T(8,128)(2,1)S(1)}, u32[]{:S(2)}, u32[]{:S(2)}) %collective-permute-start.31) | collective-permute-done | bytes 262176 | tf_op jit(solution)/shard_map/ppermute | solution.py:59
  151.1 3.6 %collective-permute-done.20.refs_9_ = bf16[128,1024]{1,0:T(8,128)(2,1)S(1)} collective-permute-done((bf16[128,1024]{1,0:T(8,128)(2,1)S(1)}, bf16[128,1024]{1,0:T(8,128)(2,1)S(1)}, u32[]{:S(2)}, u32[]{:S(2)}) %collective-permute-start.20) | collective-permute-done | bytes 262176 | tf_op jit(solution)/shard_map/ppermute | solution.py:59
  156.7 3.6 %collective-permute-done.33.refs_20_ = bf16[128,1024]{1,0:T(8,128)(2,1)S(1)} collective-permute-done((bf16[128,1024]{1,0:T(8,128)(2,1)S(1)}, bf16[128,1024]{1,0:T(8,128)(2,1)S(1)}, u32[]{:S(2)}, u32[]{:S(2)}) %collective-permute-start.33) | collective-permute-done | bytes 262176 | tf_op jit(solution)/shard_map/ppermute | solution.py:59
  162.4 3.5 %collective-permute-done.22.refs_11_ = bf16[128,1024]{1,0:T(8,128)(2,1)S(1)} collective-permute-done((bf16[128,1024]{1,0:T(8,128)(2,1)S(1)}, bf16[128,1024]{1,0:T(8,128)(2,1)S(1)}, u32[]{:S(2)}, u32[]{:S(2)}) %collective-permute-start.22) | collective-permute-done | bytes 262176 | tf_op jit(solution)/shard_map/ppermute | solution.py:59
  169.0 1.9 collective-permute-done.24.refs_13_
  170.9 1.6 collective-permute-done.23.refs_12_
  173.3 13.1 %attention.1 = (bf16[8,4,2,64,128]{4,3,2,1,0:T(8,128)(2,1)}, bf16[4096,128]{1,0:T(8,128)(2,1)}) custom-call(s32[2]{0:T(128)} %pad_add_fusion.refs_0_, s32[2,8]{1,0:T(2,128)} %constant.56.clone.refs_1_, s32[2]{0:T(128)} %refs_2_.3, bf16[8,4,2,64,128]{4,3,2,1,0:T(8,128)(2,1)} %copy-done.3, bf16[2048,256]{1,0:T(8,128)(2,1)} %bitcast.40, ...), custom_call_target="tpu_custom_call" | custom-call | tf_op jit(solution)/shard_map/attention/pallas_call | solution.py:422
  187.8 5.1 %all-to-all-start.1 = ((bf16[8,4,2,64,128]{4,3,2,1,0:T(8,128)(2,1)}), bf16[8,4,2,64,128]{4,3,2,1,0:T(8,128)(2,1)S(1)}, u32[]{:S(2)}, u32[]{:S(2)}) async-start(bf16[8,4,2,64,128]{4,3,2,1,0:T(8,128)(2,1)} %get-tuple-element.51), calls=%async_computation.1 | async-start | bytes 2097152 | tf_op jit(solution)/shard_map/all_to_all | solution.py:491
  192.9 15.3 %collective-permute-done.36 = bf16[4096,128]{1,0:T(8,128)(2,1)} collective-permute-done((bf16[4096,128]{1,0:T(8,128)(2,1)}, bf16[4096,128]{1,0:T(8,128)(2,1)}, u32[]{:S(2)}, u32[]{:S(2)}) %collective-permute-start.36) | collective-permute-done | bytes 1048608 | tf_op jit(solution)/shard_map/ppermute | solution.py:76
  209.8 5.8 %all-to-all-done.1.packed = bf16[8,4,2,64,128]{4,3,2,1,0:T(8,128)(2,1)S(1)} async-done(((bf16[8,4,2,64,128]{4,3,2,1,0:T(8,128)(2,1)}), bf16[8,4,2,64,128]{4,3,2,1,0:T(8,128)(2,1)S(1)}, u32[]{:S(2)}, u32[]{:S(2)}) %all-to-all-start.1) | async-done | bytes 1048608 | tf_op jit(solution)/shard_map/all_to_all | solution.py:491
  216.5 2.5 %unpack.1 = (bf16[2,64,1024]{2,1,0:T(8,128)(2,1)}, bf16[3,2,64,1024]{3,2,1,0:T(8,128)(2,1)}) custom-call(bf16[8,4,2,64,128]{4,3,2,1,0:T(8,128)(2,1)} %copy-done.2), custom_call_target="tpu_custom_call" | custom-call | tf_op jit(solution)/shard_map/unpack/pallas_call | solution.py:201
  (159 shorter events, 45.4 us)
Async XLA Ops:
  3.1 29.6 %collective-permute-start.1 = (bf16[1056,256]{1,0:T(8,128)(2,1)S(1)}, bf16[1056,256]{1,0:T(8,128)(2,1)S(1)}, u32[]{:S(2)}, u32[]{:S(2)}) collective-permute-start(bf16[1056,256]{1,0:T(8,128)(2,1)S(1)} %pad_maximum_fusion.2.refs_5_.refs_9_), channel_id=1, source_target_pairs={{0,4},{1,5},{2,6},{3,7},{4,0},{5,1},{6,2},{7,3},{8,12},{9,13},{10,... | collective-permute-start | bytes 1622024 | tf_op jit(solution)/shard_map/ppermute | solution.py:76
  7.2 25.5 %collective-permute-start = (bf16[1056,256]{1,0:T(8,128)(2,1)S(1)}, bf16[1056,256]{1,0:T(8,128)(2,1)S(1)}, u32[]{:S(2)}, u32[]{:S(2)}) collective-permute-start(bf16[1056,256]{1,0:T(8,128)(2,1)S(1)} %pad_maximum_fusion.2.refs_5_.refs_9_), channel_id=1, source_target_pairs={{0,1},{1,0},{2,3},{3,2},{4,5},{5,4},{6,7},{7,6},{8,9},{9,8},{10,11... | collective-permute-start | bytes 1622024 | tf_op jit(solution)/shard_map/ppermute | solution.py:76
  8.7 23.9 %collective-permute-start.2 = (bf16[1056,256]{1,0:T(8,128)(2,1)S(1)}, bf16[1056,256]{1,0:T(8,128)(2,1)S(1)}, u32[]{:S(2)}, u32[]{:S(2)}) collective-permute-start(bf16[1056,256]{1,0:T(8,128)(2,1)S(1)} %pad_maximum_fusion.1), channel_id=1, source_target_pairs={{0,2},{1,3},{2,0},{3,1},{4,6},{5,7},{6,4},{7,5},{8,10},{9,11},{10,... | collective-permute-start | bytes 1622024 | tf_op jit(solution)/shard_map/ppermute | solution.py:76
  32.7 28.8 %collective-permute-start.3 = (bf16[144,2048]{1,0:T(8,128)(2,1)S(1)}, bf16[144,2048]{1,0:T(8,128)(2,1)}, u32[]{:S(2)}, u32[]{:S(2)}) collective-permute-start(bf16[144,2048]{1,0:T(8,128)(2,1)S(1)} %pad_maximum_fusion.refs_1_), channel_id=1, source_target_pairs={{0,2},{1,3},{2,0},{3,1},{4,6},{5,7},{6,4},{7,5},{8,10},{9,11},{10,... | collective-permute-start | bytes 1769480 | tf_op jit(solution)/shard_map/ppermute | solution.py:76
  32.9 28.6 %collective-permute-start.4 = (bf16[144,2048]{1,0:T(8,128)(2,1)S(1)}, bf16[144,2048]{1,0:T(8,128)(2,1)S(1)}, u32[]{:S(2)}, u32[]{:S(2)}) collective-permute-start(bf16[144,2048]{1,0:T(8,128)(2,1)S(1)} %pad_maximum_fusion.refs_1_), channel_id=1, source_target_pairs={{0,16},{8,24},{16,0},{24,8},{1,17},{9,25},{17,1},{25,9},{2,18},{10... | collective-permute-start | bytes 1769480 | tf_op jit(solution)/shard_map/ppermute | solution.py:76
  34.4 25.6 %collective-permute-start.5 = (bf16[1056,256]{1,0:T(8,128)(2,1)S(1)}, bf16[1056,256]{1,0:T(8,128)(2,1)}, u32[]{:S(2)}, u32[]{:S(2)}) collective-permute-start(bf16[1056,256]{1,0:T(8,128)(2,1)S(1)} %pad_maximum_fusion.1), channel_id=1, source_target_pairs={{0,6},{1,7},{2,4},{3,5},{4,2},{5,3},{6,0},{7,1},{8,14},{9,15},{10,... | collective-permute-start | bytes 1622024 | tf_op jit(solution)/shard_map/ppermute | solution.py:76
  36.8 23.2 %collective-permute-start.6 = (bf16[1056,256]{1,0:T(8,128)(2,1)S(1)}, bf16[1056,256]{1,0:T(8,128)(2,1)S(1)}, u32[]{:S(2)}, u32[]{:S(2)}) collective-permute-start(bf16[1056,256]{1,0:T(8,128)(2,1)S(1)} %collective-permute-done.1.refs_9_.refs_13_), channel_id=1, source_target_pairs={{0,1},{1,0},{2,3},{3,2},{4,5},{5,4},{6,7},{7,6},{8,9},{9,8},{10,11... | collective-permute-start | bytes 1622024 | tf_op jit(solution)/shard_map/ppermute | solution.py:76
  37.7 23.7 %collective-permute-start.7 = (bf16[1056,256]{1,0:T(8,128)(2,1)S(1)}, bf16[1056,256]{1,0:T(8,128)(2,1)S(1)}, u32[]{:S(2)}, u32[]{:S(2)}) collective-permute-start(bf16[1056,256]{1,0:T(8,128)(2,1)S(1)} %collective-permute-done.2.refs_7_.refs_11_), channel_id=1, source_target_pairs={{0,1},{1,0},{2,3},{3,2},{4,5},{5,4},{6,7},{7,6},{8,9},{9,8},{10,11... | collective-permute-start | bytes 1622024 | tf_op jit(solution)/shard_map/ppermute | solution.py:76
  61.6 16.1 %collective-permute-start.9 = (bf16[144,2048]{1,0:T(8,128)(2,1)}, bf16[144,2048]{1,0:T(8,128)(2,1)}, u32[]{:S(2)}, u32[]{:S(2)}) collective-permute-start(bf16[144,2048]{1,0:T(8,128)(2,1)} %collective-permute-done.3.refs_5_), channel_id=1, source_target_pairs={{0,16},{8,24},{16,0},{24,8},{1,17},{9,25},{17,1},{25,9},{2,18},{10... | collective-permute-start | bytes 1769480 | tf_op jit(solution)/shard_map/ppermute | solution.py:76
  62.3 14.5 %collective-permute-start.8 = (bf16[1056,256]{1,0:T(8,128)(2,1)}, bf16[1056,256]{1,0:T(8,128)(2,1)S(1)}, u32[]{:S(2)}, u32[]{:S(2)}) collective-permute-start(bf16[1056,256]{1,0:T(8,128)(2,1)} %collective-permute-done.5.refs_15_), channel_id=1, source_target_pairs={{0,1},{1,0},{2,3},{3,2},{4,5},{5,4},{6,7},{7,6},{8,9},{9,8},{10,11... | collective-permute-start | bytes 1622024 | tf_op jit(solution)/shard_map/ppermute | solution.py:76
  64.3 16.9 %collective-permute-start.12 = (bf16[144,2048]{1,0:T(8,128)(2,1)}, bf16[144,2048]{1,0:T(8,128)(2,1)}, u32[]{:S(2)}, u32[]{:S(2)}) collective-permute-start(bf16[144,2048]{1,0:T(8,128)(2,1)} %collective-permute-done.3.refs_5_), channel_id=1, source_target_pairs={{0,8},{8,0},{16,24},{24,16},{1,9},{9,1},{17,25},{25,17},{2,10},{10... | collective-permute-start | bytes 1769480 | tf_op jit(solution)/shard_map/ppermute | solution.py:76
  77.6 30.3 %all-to-all-start = ((bf16[8,4,2,64,128]{4,3,2,1,0:T(8,128)(2,1)}), bf16[8,4,2,64,128]{4,3,2,1,0:T(8,128)(2,1)S(1)}, u32[]{:S(2)}, u32[]{:S(2)}) async-start(bf16[8,4,2,64,128]{4,3,2,1,0:T(8,128)(2,1)} %pack.1), calls=%async_computation | async-start | bytes 2097152 | tf_op jit(solution)/shard_map/all_to_all | solution.py:479
  98.5 19.1 %collective-permute-start.26 = (bf16[1,2,128,1024]{3,2,1,0:T(8,128)(2,1)}, bf16[1,2,128,1024]{3,2,1,0:T(8,128)(2,1)}, u32[]{:S(2)}, u32[]{:S(2)}) collective-permute-start(bf16[1,2,128,1024]{3,2,1,0:T(8,128)(2,1)} %add_convert_fusion.1), channel_id=1, source_target_pairs={{0,2},{1,3},{2,0},{3,1},{4,6},{5,7},{6,4},{7,5},{8,10},{9,11},{10,... | collective-permute-start | bytes 1572872 | tf_op jit(solution)/shard_map/ppermute | solution.py:76
  108.0 14.4 %collective-permute-start.15 = (bf16[2,1,128,1024]{3,2,1,0:T(8,128)(2,1)}, bf16[2,1,128,1024]{3,2,1,0:T(8,128)(2,1)S(1)}, u32[]{:S(2)}, u32[]{:S(2)}) collective-permute-start(bf16[2,1,128,1024]{3,2,1,0:T(8,128)(2,1)} %add_convert_fusion.2), channel_id=1, source_target_pairs={{0,16},{8,24},{16,0},{24,8},{1,17},{9,25},{17,1},{25,9},{2,18},{10... | collective-permute-start | bytes 1572872 | tf_op jit(solution)/shard_map/ppermute | solution.py:76
  118.7 8.6 %collective-permute-start.27 = (bf16[1,1,128,1024]{3,2,1,0:T(8,128)(2,1)S(1)}, bf16[1,1,128,1024]{3,2,1,0:T(8,128)(2,1)S(1)}, u32[]{:S(2)}, u32[]{:S(2)}) collective-permute-start(bf16[1,1,128,1024]{3,2,1,0:T(8,128)(2,1)S(1)} %add_convert_fusion.4), channel_id=1, source_target_pairs={{0,16},{8,24},{16,0},{24,8},{1,17},{9,25},{17,1},{25,9},{2,18},{10... | collective-permute-start | bytes 786440 | tf_op jit(solution)/shard_map/ppermute | solution.py:76
  122.5 8.1 %collective-permute-start.16 = (bf16[1,1,128,1024]{3,2,1,0:T(8,128)(2,1)S(1)}, bf16[1,1,128,1024]{3,2,1,0:T(8,128)(2,1)S(1)}, u32[]{:S(2)}, u32[]{:S(2)}) collective-permute-start(bf16[1,1,128,1024]{3,2,1,0:T(8,128)(2,1)S(1)} %add_convert_fusion.6), channel_id=1, source_target_pairs={{0,2},{1,3},{2,0},{3,1},{4,6},{5,7},{6,4},{7,5},{8,10},{9,11},{10,... | collective-permute-start | bytes 786440 | tf_op jit(solution)/shard_map/ppermute | solution.py:76
  128.5 9.3 %collective-permute-start.29 = (bf16[128,1024]{1,0:T(8,128)(2,1)S(1)}, bf16[128,1024]{1,0:T(8,128)(2,1)S(1)}, u32[]{:S(2)}, u32[]{:S(2)}) collective-permute-start(bf16[128,1024]{1,0:T(8,128)(2,1)S(1)} %fusion.1.refs_14_), channel_id=1, source_target_pairs={{0,1},{2,0},{4,2},{6,4},{7,6},{5,7},{3,5},{1,3},{8,9},{10,8},{12,1... | collective-permute-start | bytes 786440 | tf_op jit(solution)/shard_map/ppermute | solution.py:59
  130.0 9.2 %collective-permute-start.28 = (bf16[128,1024]{1,0:T(8,128)(2,1)S(1)}, bf16[128,1024]{1,0:T(8,128)(2,1)S(1)}, u32[]{:S(2)}, u32[]{:S(2)}) collective-permute-start(bf16[128,1024]{1,0:T(8,128)(2,1)S(1)} %fusion.1.refs_14_), channel_id=1, source_target_pairs={{0,2},{2,4},{4,6},{6,7},{7,5},{5,3},{3,1},{1,0},{8,10},{10,12},{12... | collective-permute-start | bytes 786440 | tf_op jit(solution)/shard_map/ppermute | solution.py:58
  130.8 12.6 %collective-permute-start.18 = (bf16[128,1024]{1,0:T(8,128)(2,1)S(1)}, bf16[128,1024]{1,0:T(8,128)(2,1)S(1)}, u32[]{:S(2)}, u32[]{:S(2)}) collective-permute-start(bf16[128,1024]{1,0:T(8,128)(2,1)S(1)} %fusion.refs_5_), channel_id=1, source_target_pairs={{0,1},{2,0},{4,2},{6,4},{7,6},{5,7},{3,5},{1,3},{8,9},{10,8},{12,1... | collective-permute-start | bytes 786440 | tf_op jit(solution)/shard_map/ppermute | solution.py:59
  132.3 12.6 %collective-permute-start.17 = (bf16[128,1024]{1,0:T(8,128)(2,1)S(1)}, bf16[128,1024]{1,0:T(8,128)(2,1)S(1)}, u32[]{:S(2)}, u32[]{:S(2)}) collective-permute-start(bf16[128,1024]{1,0:T(8,128)(2,1)S(1)} %fusion.refs_5_), channel_id=1, source_target_pairs={{0,2},{2,4},{4,6},{6,7},{7,5},{5,3},{3,1},{1,0},{8,10},{10,12},{12... | collective-permute-start | bytes 786440 | tf_op jit(solution)/shard_map/ppermute | solution.py:58
  137.8 11.2 %collective-permute-start.31 = (bf16[128,1024]{1,0:T(8,128)(2,1)S(1)}, bf16[128,1024]{1,0:T(8,128)(2,1)S(1)}, u32[]{:S(2)}, u32[]{:S(2)}) collective-permute-start(bf16[128,1024]{1,0:T(8,128)(2,1)S(1)} %collective-permute-done.29.refs_16_), channel_id=1, source_target_pairs={{0,1},{2,0},{4,2},{6,4},{7,6},{5,7},{3,5},{1,3},{8,9},{10,8},{12,1... | collective-permute-start | bytes 786440 | tf_op jit(solution)/shard_map/ppermute | solution.py:59
  139.3 11.2 %collective-permute-start.30 = (bf16[128,1024]{1,0:T(8,128)(2,1)S(1)}, bf16[128,1024]{1,0:T(8,128)(2,1)S(1)}, u32[]{:S(2)}, u32[]{:S(2)}) collective-permute-start(bf16[128,1024]{1,0:T(8,128)(2,1)S(1)} %collective-permute-done.28.refs_15_), channel_id=1, source_target_pairs={{0,2},{2,4},{4,6},{6,7},{7,5},{5,3},{3,1},{1,0},{8,10},{10,12},{12... | collective-permute-start | bytes 786440 | tf_op jit(solution)/shard_map/ppermute | solution.py:58
  143.4 11.2 %collective-permute-start.20 = (bf16[128,1024]{1,0:T(8,128)(2,1)S(1)}, bf16[128,1024]{1,0:T(8,128)(2,1)S(1)}, u32[]{:S(2)}, u32[]{:S(2)}) collective-permute-start(bf16[128,1024]{1,0:T(8,128)(2,1)S(1)} %collective-permute-done.18.refs_7_), channel_id=1, source_target_pairs={{0,1},{2,0},{4,2},{6,4},{7,6},{5,7},{3,5},{1,3},{8,9},{10,8},{12,1... | collective-permute-start | bytes 786440 | tf_op jit(solution)/shard_map/ppermute | solution.py:59
  144.9 11.2 %collective-permute-start.19 = (bf16[128,1024]{1,0:T(8,128)(2,1)S(1)}, bf16[128,1024]{1,0:T(8,128)(2,1)S(1)}, u32[]{:S(2)}, u32[]{:S(2)}) collective-permute-start(bf16[128,1024]{1,0:T(8,128)(2,1)S(1)} %collective-permute-done.17.refs_6_), channel_id=1, source_target_pairs={{0,2},{2,4},{4,6},{6,7},{7,5},{5,3},{3,1},{1,0},{8,10},{10,12},{12... | collective-permute-start | bytes 786440 | tf_op jit(solution)/shard_map/ppermute | solution.py:58
  149.0 11.2 %collective-permute-start.33 = (bf16[128,1024]{1,0:T(8,128)(2,1)S(1)}, bf16[128,1024]{1,0:T(8,128)(2,1)S(1)}, u32[]{:S(2)}, u32[]{:S(2)}) collective-permute-start(bf16[128,1024]{1,0:T(8,128)(2,1)S(1)} %collective-permute-done.31.refs_18_), channel_id=1, source_target_pairs={{0,1},{2,0},{4,2},{6,4},{7,6},{5,7},{3,5},{1,3},{8,9},{10,8},{12,1... | collective-permute-start | bytes 786440 | tf_op jit(solution)/shard_map/ppermute | solution.py:59
  150.5 11.3 %collective-permute-start.32 = (bf16[128,1024]{1,0:T(8,128)(2,1)S(1)}, bf16[128,1024]{1,0:T(8,128)(2,1)S(1)}, u32[]{:S(2)}, u32[]{:S(2)}) collective-permute-start(bf16[128,1024]{1,0:T(8,128)(2,1)S(1)} %collective-permute-done.30.refs_17_), channel_id=1, source_target_pairs={{0,2},{2,4},{4,6},{6,7},{7,5},{5,3},{3,1},{1,0},{8,10},{10,12},{12... | collective-permute-start | bytes 786440 | tf_op jit(solution)/shard_map/ppermute | solution.py:58
  154.7 11.2 %collective-permute-start.22 = (bf16[128,1024]{1,0:T(8,128)(2,1)S(1)}, bf16[128,1024]{1,0:T(8,128)(2,1)S(1)}, u32[]{:S(2)}, u32[]{:S(2)}) collective-permute-start(bf16[128,1024]{1,0:T(8,128)(2,1)S(1)} %collective-permute-done.20.refs_9_), channel_id=1, source_target_pairs={{0,1},{2,0},{4,2},{6,4},{7,6},{5,7},{3,5},{1,3},{8,9},{10,8},{12,1... | collective-permute-start | bytes 786440 | tf_op jit(solution)/shard_map/ppermute | solution.py:59
  156.1 11.1 %collective-permute-start.21 = (bf16[128,1024]{1,0:T(8,128)(2,1)S(1)}, bf16[128,1024]{1,0:T(8,128)(2,1)S(1)}, u32[]{:S(2)}, u32[]{:S(2)}) collective-permute-start(bf16[128,1024]{1,0:T(8,128)(2,1)S(1)} %collective-permute-done.19.refs_8_), channel_id=1, source_target_pairs={{0,2},{2,4},{4,6},{6,7},{7,5},{5,3},{3,1},{1,0},{8,10},{10,12},{12... | collective-permute-start | bytes 786440 | tf_op jit(solution)/shard_map/ppermute | solution.py:58
  160.3 8.2 %collective-permute-start.35 = (bf16[64,1024]{1,0:T(8,128)(2,1)S(1)}, bf16[64,1024]{1,0:T(8,128)(2,1)S(1)}, u32[]{:S(2)}, u32[]{:S(2)}) collective-permute-start(bf16[64,1024]{1,0:T(8,128)(2,1)S(1)} %slice.115), channel_id=1, source_target_pairs={{0,1},{2,0},{4,2},{6,4},{7,6},{5,7},{3,5},{1,3},{8,9},{10,8},{12,1... | collective-permute-start | bytes 393224 | tf_op jit(solution)/shard_map/ppermute | solution.py:63
  186.3 21.9 %collective-permute-start.36 = (bf16[4096,128]{1,0:T(8,128)(2,1)}, bf16[4096,128]{1,0:T(8,128)(2,1)}, u32[]{:S(2)}, u32[]{:S(2)}) collective-permute-start(bf16[4096,128]{1,0:T(8,128)(2,1)} %get-tuple-element.54), channel_id=1, source_target_pairs={{0,16},{8,24},{16,0},{24,8},{1,17},{9,25},{17,1},{25,9},{2,18},{10... | collective-permute-start | bytes 3145736 | tf_op jit(solution)/shard_map/ppermute | solution.py:76
  187.8 27.7 %all-to-all-start.1 = ((bf16[8,4,2,64,128]{4,3,2,1,0:T(8,128)(2,1)}), bf16[8,4,2,64,128]{4,3,2,1,0:T(8,128)(2,1)S(1)}, u32[]{:S(2)}, u32[]{:S(2)}) async-start(bf16[8,4,2,64,128]{4,3,2,1,0:T(8,128)(2,1)} %get-tuple-element.51), calls=%async_computation.1 | async-start | bytes 2097152 | tf_op jit(solution)/shard_map/all_to_all | solution.py:491
  209.7 9.3 %collective-permute-start.37 = (bf16[4096,128]{1,0:T(8,128)(2,1)S(1)}, bf16[4096,128]{1,0:T(8,128)(2,1)S(1)}, u32[]{:S(2)}, u32[]{:S(2)}) collective-permute-start(bf16[4096,128]{1,0:T(8,128)(2,1)S(1)} %add_convert_fusion), channel_id=1, source_target_pairs={{0,8},{8,0},{16,24},{24,16},{1,9},{9,1},{17,25},{25,17},{2,10},{10... | collective-permute-start | bytes 3145736 | tf_op jit(solution)/shard_map/ppermute | solution.py:76
  (50 other events, 639.7 us)

commit v3 on v0

--- a/solution.py
+++ b/solution.py
@@ -185,27 +185,10 @@
     )(*arrays)
 
 
-def unpack_body(packed, attended, grads):
-    for head in range(packed.shape[0]):
-        cols = slice(head * HD, (head + 1) * HD)
-        attended[:, :, cols] = packed[head, 0]
-        for which in range(3):
-            grads[which, :, :, cols] = packed[head, which + 1]
-
-
 def unpack(packed):
-    heads, _, pages, rows, _ = packed.shape
-    return pl.pallas_call(
-        unpack_body,
-        out_shape=(
-            jax.ShapeDtypeStruct((pages, rows, heads * HD), BF16),
-            jax.ShapeDtypeStruct((3, pages, rows, heads * HD), BF16),
-        ),
-        in_specs=[vmem()],
-        out_specs=(vmem(), vmem()),
-        compiler_params=params(),
-        name="unpack",
-    )(packed)
+    heads = range(packed.shape[0])
+    attended = jnp.concatenate([packed[head, 0] for head in heads], axis=-1)
+    return attended, jnp.concatenate([packed[head, 1:] for head in heads], axis=-1)
 
 
 def with_gates(rows, expert_ids, expert_gates):

time: 218 us -> 215 us (0.986)
  Pallas kernels: 34.1 us -> 31.6 us
    pallas_call x1 -> x0, Pallas kernels: 2.49 us -> none  [unpack(): pl.pallas_call(unpack_body, out_shape=(jax.ShapeDtypeStruct((pages, rows,...]
    unnamed x81 -> x97, local copies, waits for them, and re-layouts: 6.49 us -> 5.81 us
  transfers between devices with their start and end apart: 40 -> 40, of which waited for: 21 -> 21; matrix products, arithmetic and copies ran while one was open for 4% -> 4% of each run, Pallas kernels for 10% -> 9%
where the time goes in v3:
time: 215 us
  waiting for transfers between devices  118 us (55%)
  starting transfers between devices  46.4 us (22%)
  Pallas kernels  31.6 us (15%)
  other arithmetic  8.9 us (4%)
  local copies, waits for them, and re-layouts  8.27 us (4%)
    ppermute x22, waiting for transfers between devices, xor_swap(): return lax.ppermute(array, axis, [(i, i ^ mask) for i in range(count)])  80.3 us
    ppermute x6, waiting for transfers between devices, ring_gather(): down = lax.ppermute(down, 'seq', back)  22.6 us
    ppermute x22, starting transfers between devices, xor_swap(): return lax.ppermute(array, axis, [(i, i ^ mask) for i in range(count)])  22.3 us
    pallas_call x1, Pallas kernels, attention_stage(): pl.pallas_call(body, out_shape=(jax.ShapeDtypeStruct(latents.shape, BF16)...  13.1 us
    pallas_call x1, Pallas kernels, expert_stage(): pl.pallas_call(body, out_shape=(shape,) * 4, in_specs=[smem()] + [vmem()]...  11 us
    ppermute x6, starting transfers between devices, ring_gather(): down = lax.ppermute(down, 'seq', back)  8.95 us
    all_to_all x1, waiting for transfers between devices, local(): lax.all_to_all(packed, 'seq', split_axis=0, concat_axis=0, tiled=True)  5.84 us
    unnamed x97, local copies, waits for them, and re-layouts  5.81 us
  transfers between devices with their start and end apart: 40, of which 21 were waited for; matrix products, arithmetic and copies ran while one was open for 4% of the time, Pallas kernels for 9%

profile of v3, /device:TPU:0, one launch (start us, length us, event | category | flops | bytes accessed | tf_op | source)
XLA Modules:
  0.0 214.8 jit_solution(14892732910097349497)
XLA Ops:
  3.1 4.1 %collective-permute-start.1 = (bf16[1056,256]{1,0:T(8,128)(2,1)S(1)}, bf16[1056,256]{1,0:T(8,128)(2,1)S(1)}, u32[]{:S(2)}, u32[]{:S(2)}) collective-permute-start(bf16[1056,256]{1,0:T(8,128)(2,1)S(1)} %pad_maximum_fusion.2.refs_5_.refs_9_), channel_id=1, source_target_pairs={{0,4},{1,5},{2,6},{3,7},{4,0},{5,1},{6,2},{7,3},{8,12},{9,13},{10,... | collective-permute-start | bytes 1622024 | tf_op jit(solution)/shard_map/ppermute | solution.py:76
  8.7 1.6 collective-permute-start.2
  11.5 2.4 %pack.1 = bf16[8,4,2,64,128]{4,3,2,1,0:T(8,128)(2,1)} custom-call(bf16[2,64,1024]{2,1,0:T(8,128)(2,1)} %refs_0_.1, bf16[2,64,1024]{2,1,0:T(8,128)(2,1)} %refs_1_.2, bf16[2,64,1024]{2,1,0:T(8,128)(2,1)} %refs_2_.2, bf16[2,64,1024]{2,1,0:T(8,128)(2,1)} %refs_3_.1), custom_call_target="tpu_custom_call" | custom-call | tf_op jit(solution)/shard_map/pack/pallas_call | solution.py:178
  14.0 18.6 %collective-permute-done.2.refs_7_.refs_11_ = bf16[1056,256]{1,0:T(8,128)(2,1)S(1)} collective-permute-done((bf16[1056,256]{1,0:T(8,128)(2,1)S(1)}, bf16[1056,256]{1,0:T(8,128)(2,1)S(1)}, u32[]{:S(2)}, u32[]{:S(2)}) %collective-permute-start.2) | collective-permute-done | bytes 540704 | tf_op jit(solution)/shard_map/ppermute | solution.py:76
  34.4 2.4 %collective-permute-start.5 = (bf16[1056,256]{1,0:T(8,128)(2,1)S(1)}, bf16[1056,256]{1,0:T(8,128)(2,1)}, u32[]{:S(2)}, u32[]{:S(2)}) collective-permute-start(bf16[1056,256]{1,0:T(8,128)(2,1)S(1)} %pad_maximum_fusion.1), channel_id=1, source_target_pairs={{0,6},{1,7},{2,4},{3,5},{4,2},{5,3},{6,0},{7,1},{8,14},{9,15},{10,... | collective-permute-start | bytes 1622024 | tf_op jit(solution)/shard_map/ppermute | solution.py:76
  38.8 21.1 %collective-permute-done.5.refs_15_ = bf16[1056,256]{1,0:T(8,128)(2,1)} collective-permute-done((bf16[1056,256]{1,0:T(8,128)(2,1)S(1)}, bf16[1056,256]{1,0:T(8,128)(2,1)}, u32[]{:S(2)}, u32[]{:S(2)}) %collective-permute-start.5) | collective-permute-done | bytes 540704 | tf_op jit(solution)/shard_map/ppermute | solution.py:76
  66.0 5.1 %hidden_sums.1.refs_17_ = f32[512,704]{1,0:T(8,128)} custom-call(s32[2]{0:T(128)} %pad_add_fusion.refs_0_, bf16[144,2048]{1,0:T(8,128)(2,1)} %copy-done, bf16[144,2048]{1,0:T(8,128)(2,1)} %copy-done.4, bf16[144,2048]{1,0:T(8,128)(2,1)} %copy-done.3, bf16[144,2048]{1,0:T(8,128)(2,1)} %copy-done.5, bf16[1056,256]{1,0:T(8,128)(2,1)} %copy-done.1, ...), custom_call_target="tpu_custom_call" | custom-call | tf_op jit(solution)/shard_map/hidden_sums/pallas_call | solution.py:237
  71.2 5.6 %collective-permute-done.8.refs_16_ = bf16[1056,256]{1,0:T(8,128)(2,1)S(1)} collective-permute-done((bf16[1056,256]{1,0:T(8,128)(2,1)}, bf16[1056,256]{1,0:T(8,128)(2,1)S(1)}, u32[]{:S(2)}, u32[]{:S(2)}) %collective-permute-start.8) | collective-permute-done | bytes 540704 | tf_op jit(solution)/shard_map/ppermute | solution.py:76
  77.6 3.6 %all-to-all-start = ((bf16[8,4,2,64,128]{4,3,2,1,0:T(8,128)(2,1)}), bf16[8,4,2,64,128]{4,3,2,1,0:T(8,128)(2,1)S(1)}, u32[]{:S(2)}, u32[]{:S(2)}) async-start(bf16[8,4,2,64,128]{4,3,2,1,0:T(8,128)(2,1)} %pack.1), calls=%async_computation | async-start | bytes 2097152 | tf_op jit(solution)/shard_map/all_to_all | solution.py:459
  82.0 11.0 %expert.1 = (bf16[2,2,128,1024]{3,2,1,0:T(8,128)(2,1)}, bf16[2,2,128,1024]{3,2,1,0:T(8,128)(2,1)}, bf16[2,2,128,1024]{3,2,1,0:T(8,128)(2,1)}, bf16[2,2,128,1024]{3,2,1,0:T(8,128)(2,1)}) custom-call(s32[2]{0:T(128)} %pad_add_fusion.refs_0_, bf16[144,2048]{1,0:T(8,128)(2,1)} %copy-done, bf16[144,2048]{1,0:T(8,128)(2,1)} %copy-done.4, ...), custom_call_target="tpu_custom_call" | custom-call | tf_op jit(solution)/shard_map/expert/pallas_call | solution.py:298
  93.6 2.4 %collective-permute-done.14 = bf16[2,2,128,1024]{3,2,1,0:T(8,128)(2,1)S(1)} collective-permute-done((bf16[2,2,128,1024]{3,2,1,0:T(8,128)(2,1)}, bf16[2,2,128,1024]{3,2,1,0:T(8,128)(2,1)S(1)}, u32[]{:S(2)}, u32[]{:S(2)}) %collective-permute-start.14) | collective-permute-done | bytes 1048608 | tf_op jit(solution)/shard_map/ppermute | solution.py:76
  96.1 1.6 convert_add_fusion.2
  102.0 5.8 %all-to-all-done.refs_3_ = bf16[8,4,2,64,128]{4,3,2,1,0:T(8,128)(2,1)S(1)} async-done(((bf16[8,4,2,64,128]{4,3,2,1,0:T(8,128)(2,1)}), bf16[8,4,2,64,128]{4,3,2,1,0:T(8,128)(2,1)S(1)}, u32[]{:S(2)}, u32[]{:S(2)}) %all-to-all-start) | async-done | bytes 1048608 | tf_op jit(solution)/shard_map/all_to_all | solution.py:459
  107.9 5.2 %collective-permute-done.15 = bf16[2,1,128,1024]{3,2,1,0:T(8,128)(2,1)} collective-permute-done((bf16[2,1,128,1024]{3,2,1,0:T(8,128)(2,1)}, bf16[2,1,128,1024]{3,2,1,0:T(8,128)(2,1)}, u32[]{:S(2)}, u32[]{:S(2)}) %collective-permute-start.15) | collective-permute-done | bytes 524320 | tf_op jit(solution)/shard_map/ppermute | solution.py:76
  114.3 1.7 collective-permute-start.16
  116.0 6.9 %collective-permute-done.26 = bf16[2,128,1024]{2,1,0:T(8,128)(2,1)S(1)} collective-permute-done((bf16[2,128,1024]{2,1,0:T(8,128)(2,1)}, bf16[2,128,1024]{2,1,0:T(8,128)(2,1)S(1)}, u32[]{:S(2)}, u32[]{:S(2)}) %collective-permute-start.26) | collective-permute-done | bytes 524320 | tf_op jit(solution)/shard_map/ppermute | solution.py:76
  124.7 2.6 %collective-permute-done.16 = bf16[1,128,1024]{2,1,0:T(8,128)(2,1)S(1)} collective-permute-done((bf16[1,128,1024]{2,1,0:T(8,128)(2,1)S(1)}, bf16[1,128,1024]{2,1,0:T(8,128)(2,1)S(1)}, u32[]{:S(2)}, u32[]{:S(2)}) %collective-permute-start.16) | collective-permute-done | bytes 262176 | tf_op jit(solution)/shard_map/ppermute | solution.py:76
  127.3 1.5 collective-permute-start.18
  131.8 4.8 %collective-permute-done.18.refs_7_ = bf16[128,1024]{1,0:T(8,128)(2,1)S(1)} collective-permute-done((bf16[128,1024]{1,0:T(8,128)(2,1)S(1)}, bf16[128,1024]{1,0:T(8,128)(2,1)S(1)}, u32[]{:S(2)}, u32[]{:S(2)}) %collective-permute-start.18) | collective-permute-done | bytes 262176 | tf_op jit(solution)/shard_map/ppermute | solution.py:59
  138.7 3.6 %collective-permute-done.29.refs_16_ = bf16[128,1024]{1,0:T(8,128)(2,1)S(1)} collective-permute-done((bf16[128,1024]{1,0:T(8,128)(2,1)S(1)}, bf16[128,1024]{1,0:T(8,128)(2,1)S(1)}, u32[]{:S(2)}, u32[]{:S(2)}) %collective-permute-start.29) | collective-permute-done | bytes 262176 | tf_op jit(solution)/shard_map/ppermute | solution.py:59
  144.3 3.6 %collective-permute-done.20.refs_9_ = bf16[128,1024]{1,0:T(8,128)(2,1)S(1)} collective-permute-done((bf16[128,1024]{1,0:T(8,128)(2,1)S(1)}, bf16[128,1024]{1,0:T(8,128)(2,1)S(1)}, u32[]{:S(2)}, u32[]{:S(2)}) %collective-permute-start.20) | collective-permute-done | bytes 262176 | tf_op jit(solution)/shard_map/ppermute | solution.py:59
  149.9 3.6 %collective-permute-done.31.refs_18_ = bf16[128,1024]{1,0:T(8,128)(2,1)S(1)} collective-permute-done((bf16[128,1024]{1,0:T(8,128)(2,1)S(1)}, bf16[128,1024]{1,0:T(8,128)(2,1)S(1)}, u32[]{:S(2)}, u32[]{:S(2)}) %collective-permute-start.31) | collective-permute-done | bytes 262176 | tf_op jit(solution)/shard_map/ppermute | solution.py:59
  155.5 3.6 %collective-permute-done.22.refs_11_ = bf16[128,1024]{1,0:T(8,128)(2,1)S(1)} collective-permute-done((bf16[128,1024]{1,0:T(8,128)(2,1)S(1)}, bf16[128,1024]{1,0:T(8,128)(2,1)S(1)}, u32[]{:S(2)}, u32[]{:S(2)}) %collective-permute-start.22) | collective-permute-done | bytes 262176 | tf_op jit(solution)/shard_map/ppermute | solution.py:59
  161.3 3.5 %collective-permute-done.33.refs_20_ = bf16[128,1024]{1,0:T(8,128)(2,1)S(1)} collective-permute-done((bf16[128,1024]{1,0:T(8,128)(2,1)S(1)}, bf16[128,1024]{1,0:T(8,128)(2,1)S(1)}, u32[]{:S(2)}, u32[]{:S(2)}) %collective-permute-start.33) | collective-permute-done | bytes 262176 | tf_op jit(solution)/shard_map/ppermute | solution.py:59
  164.7 1.5 collective-permute-start.35
  167.9 1.8 collective-permute-done.35.refs_22_
  169.8 1.8 collective-permute-done.34.refs_21_
  171.7 13.1 %attention.1 = (bf16[8,4,2,64,128]{4,3,2,1,0:T(8,128)(2,1)}, bf16[4096,128]{1,0:T(8,128)(2,1)}) custom-call(s32[2]{0:T(128)} %pad_add_fusion.refs_0_, s32[2,8]{1,0:T(2,128)} %constant.56.clone.refs_1_, s32[2]{0:T(128)} %refs_2_.3, bf16[8,4,2,64,128]{4,3,2,1,0:T(8,128)(2,1)} %copy-done.2, bf16[2048,256]{1,0:T(8,128)(2,1)} %bitcast.123, ...), custom_call_target="tpu_custom_call" | custom-call | tf_op jit(solution)/shard_map/attention/pallas_call | solution.py:402
  186.3 3.9 %all-to-all-start.1 = ((bf16[8,4,2,64,128]{4,3,2,1,0:T(8,128)(2,1)}), bf16[8,4,2,64,128]{4,3,2,1,0:T(8,128)(2,1)S(1)}, u32[]{:S(2)}, u32[]{:S(2)}) async-start(bf16[8,4,2,64,128]{4,3,2,1,0:T(8,128)(2,1)} %get-tuple-element.51), calls=%async_computation.1 | async-start | bytes 2097152 | tf_op jit(solution)/shard_map/all_to_all | solution.py:471
  190.2 16.0 %collective-permute-done.36 = bf16[4096,128]{1,0:T(8,128)(2,1)} collective-permute-done((bf16[4096,128]{1,0:T(8,128)(2,1)}, bf16[4096,128]{1,0:T(8,128)(2,1)}, u32[]{:S(2)}, u32[]{:S(2)}) %collective-permute-start.36) | collective-permute-done | bytes 1048608 | tf_op jit(solution)/shard_map/ppermute | solution.py:76
  207.8 5.0 %all-to-all-done.1 = bf16[8,4,2,64,128]{4,3,2,1,0:T(8,128)(2,1)S(1)} async-done(((bf16[8,4,2,64,128]{4,3,2,1,0:T(8,128)(2,1)}), bf16[8,4,2,64,128]{4,3,2,1,0:T(8,128)(2,1)S(1)}, u32[]{:S(2)}, u32[]{:S(2)}) %all-to-all-start.1) | async-done | bytes 1048608 | tf_op jit(solution)/shard_map/all_to_all | solution.py:471
  213.3 1.6 convert_add_fusion
  (177 shorter events, 42.7 us)
Async XLA Ops:
  3.1 29.6 %collective-permute-start.1 = (bf16[1056,256]{1,0:T(8,128)(2,1)S(1)}, bf16[1056,256]{1,0:T(8,128)(2,1)S(1)}, u32[]{:S(2)}, u32[]{:S(2)}) collective-permute-start(bf16[1056,256]{1,0:T(8,128)(2,1)S(1)} %pad_maximum_fusion.2.refs_5_.refs_9_), channel_id=1, source_target_pairs={{0,4},{1,5},{2,6},{3,7},{4,0},{5,1},{6,2},{7,3},{8,12},{9,13},{10,... | collective-permute-start | bytes 1622024 | tf_op jit(solution)/shard_map/ppermute | solution.py:76
  7.2 25.5 %collective-permute-start = (bf16[1056,256]{1,0:T(8,128)(2,1)S(1)}, bf16[1056,256]{1,0:T(8,128)(2,1)S(1)}, u32[]{:S(2)}, u32[]{:S(2)}) collective-permute-start(bf16[1056,256]{1,0:T(8,128)(2,1)S(1)} %pad_maximum_fusion.2.refs_5_.refs_9_), channel_id=1, source_target_pairs={{0,1},{1,0},{2,3},{3,2},{4,5},{5,4},{6,7},{7,6},{8,9},{9,8},{10,11... | collective-permute-start | bytes 1622024 | tf_op jit(solution)/shard_map/ppermute | solution.py:76
  8.7 23.9 %collective-permute-start.2 = (bf16[1056,256]{1,0:T(8,128)(2,1)S(1)}, bf16[1056,256]{1,0:T(8,128)(2,1)S(1)}, u32[]{:S(2)}, u32[]{:S(2)}) collective-permute-start(bf16[1056,256]{1,0:T(8,128)(2,1)S(1)} %pad_maximum_fusion.1), channel_id=1, source_target_pairs={{0,2},{1,3},{2,0},{3,1},{4,6},{5,7},{6,4},{7,5},{8,10},{9,11},{10,... | collective-permute-start | bytes 1622024 | tf_op jit(solution)/shard_map/ppermute | solution.py:76
  32.7 28.8 %collective-permute-start.3 = (bf16[144,2048]{1,0:T(8,128)(2,1)S(1)}, bf16[144,2048]{1,0:T(8,128)(2,1)}, u32[]{:S(2)}, u32[]{:S(2)}) collective-permute-start(bf16[144,2048]{1,0:T(8,128)(2,1)S(1)} %pad_maximum_fusion.refs_1_), channel_id=1, source_target_pairs={{0,2},{1,3},{2,0},{3,1},{4,6},{5,7},{6,4},{7,5},{8,10},{9,11},{10,... | collective-permute-start | bytes 1769480 | tf_op jit(solution)/shard_map/ppermute | solution.py:76
  32.9 28.6 %collective-permute-start.4 = (bf16[144,2048]{1,0:T(8,128)(2,1)S(1)}, bf16[144,2048]{1,0:T(8,128)(2,1)S(1)}, u32[]{:S(2)}, u32[]{:S(2)}) collective-permute-start(bf16[144,2048]{1,0:T(8,128)(2,1)S(1)} %pad_maximum_fusion.refs_1_), channel_id=1, source_target_pairs={{0,16},{8,24},{16,0},{24,8},{1,17},{9,25},{17,1},{25,9},{2,18},{10... | collective-permute-start | bytes 1769480 | tf_op jit(solution)/shard_map/ppermute | solution.py:76
  34.4 25.6 %collective-permute-start.5 = (bf16[1056,256]{1,0:T(8,128)(2,1)S(1)}, bf16[1056,256]{1,0:T(8,128)(2,1)}, u32[]{:S(2)}, u32[]{:S(2)}) collective-permute-start(bf16[1056,256]{1,0:T(8,128)(2,1)S(1)} %pad_maximum_fusion.1), channel_id=1, source_target_pairs={{0,6},{1,7},{2,4},{3,5},{4,2},{5,3},{6,0},{7,1},{8,14},{9,15},{10,... | collective-permute-start | bytes 1622024 | tf_op jit(solution)/shard_map/ppermute | solution.py:76
  36.8 23.2 %collective-permute-start.6 = (bf16[1056,256]{1,0:T(8,128)(2,1)S(1)}, bf16[1056,256]{1,0:T(8,128)(2,1)S(1)}, u32[]{:S(2)}, u32[]{:S(2)}) collective-permute-start(bf16[1056,256]{1,0:T(8,128)(2,1)S(1)} %collective-permute-done.1.refs_9_.refs_13_), channel_id=1, source_target_pairs={{0,1},{1,0},{2,3},{3,2},{4,5},{5,4},{6,7},{7,6},{8,9},{9,8},{10,11... | collective-permute-start | bytes 1622024 | tf_op jit(solution)/shard_map/ppermute | solution.py:76
  37.7 23.7 %collective-permute-start.7 = (bf16[1056,256]{1,0:T(8,128)(2,1)S(1)}, bf16[1056,256]{1,0:T(8,128)(2,1)S(1)}, u32[]{:S(2)}, u32[]{:S(2)}) collective-permute-start(bf16[1056,256]{1,0:T(8,128)(2,1)S(1)} %collective-permute-done.2.refs_7_.refs_11_), channel_id=1, source_target_pairs={{0,1},{1,0},{2,3},{3,2},{4,5},{5,4},{6,7},{7,6},{8,9},{9,8},{10,11... | collective-permute-start | bytes 1622024 | tf_op jit(solution)/shard_map/ppermute | solution.py:76
  61.6 16.1 %collective-permute-start.9 = (bf16[144,2048]{1,0:T(8,128)(2,1)}, bf16[144,2048]{1,0:T(8,128)(2,1)}, u32[]{:S(2)}, u32[]{:S(2)}) collective-permute-start(bf16[144,2048]{1,0:T(8,128)(2,1)} %collective-permute-done.3.refs_5_), channel_id=1, source_target_pairs={{0,16},{8,24},{16,0},{24,8},{1,17},{9,25},{17,1},{25,9},{2,18},{10... | collective-permute-start | bytes 1769480 | tf_op jit(solution)/shard_map/ppermute | solution.py:76
  62.3 14.6 %collective-permute-start.8 = (bf16[1056,256]{1,0:T(8,128)(2,1)}, bf16[1056,256]{1,0:T(8,128)(2,1)S(1)}, u32[]{:S(2)}, u32[]{:S(2)}) collective-permute-start(bf16[1056,256]{1,0:T(8,128)(2,1)} %collective-permute-done.5.refs_15_), channel_id=1, source_target_pairs={{0,1},{1,0},{2,3},{3,2},{4,5},{5,4},{6,7},{7,6},{8,9},{9,8},{10,11... | collective-permute-start | bytes 1622024 | tf_op jit(solution)/shard_map/ppermute | solution.py:76
  64.4 16.8 %collective-permute-start.12 = (bf16[144,2048]{1,0:T(8,128)(2,1)}, bf16[144,2048]{1,0:T(8,128)(2,1)}, u32[]{:S(2)}, u32[]{:S(2)}) collective-permute-start(bf16[144,2048]{1,0:T(8,128)(2,1)} %collective-permute-done.3.refs_5_), channel_id=1, source_target_pairs={{0,8},{8,0},{16,24},{24,16},{1,9},{9,1},{17,25},{25,17},{2,10},{10... | collective-permute-start | bytes 1769480 | tf_op jit(solution)/shard_map/ppermute | solution.py:76
  77.6 30.2 %all-to-all-start = ((bf16[8,4,2,64,128]{4,3,2,1,0:T(8,128)(2,1)}), bf16[8,4,2,64,128]{4,3,2,1,0:T(8,128)(2,1)S(1)}, u32[]{:S(2)}, u32[]{:S(2)}) async-start(bf16[8,4,2,64,128]{4,3,2,1,0:T(8,128)(2,1)} %pack.1), calls=%async_computation | async-start | bytes 2097152 | tf_op jit(solution)/shard_map/all_to_all | solution.py:459
  98.6 14.5 %collective-permute-start.15 = (bf16[2,1,128,1024]{3,2,1,0:T(8,128)(2,1)}, bf16[2,1,128,1024]{3,2,1,0:T(8,128)(2,1)}, u32[]{:S(2)}, u32[]{:S(2)}) collective-permute-start(bf16[2,1,128,1024]{3,2,1,0:T(8,128)(2,1)} %pad_maximum_fusion.3), channel_id=1, source_target_pairs={{0,16},{8,24},{16,0},{24,8},{1,17},{9,25},{17,1},{25,9},{2,18},{10... | collective-permute-start | bytes 1572872 | tf_op jit(solution)/shard_map/ppermute | solution.py:76
  107.9 15.0 %collective-permute-start.26 = (bf16[2,128,1024]{2,1,0:T(8,128)(2,1)}, bf16[2,128,1024]{2,1,0:T(8,128)(2,1)S(1)}, u32[]{:S(2)}, u32[]{:S(2)}) collective-permute-start(bf16[2,128,1024]{2,1,0:T(8,128)(2,1)} %fusion), channel_id=1, source_target_pairs={{0,2},{1,3},{2,0},{3,1},{4,6},{5,7},{6,4},{7,5},{8,10},{9,11},{10,... | collective-permute-start | bytes 1572872 | tf_op jit(solution)/shard_map/ppermute | solution.py:76
  114.3 12.9 %collective-permute-start.16 = (bf16[1,128,1024]{2,1,0:T(8,128)(2,1)S(1)}, bf16[1,128,1024]{2,1,0:T(8,128)(2,1)S(1)}, u32[]{:S(2)}, u32[]{:S(2)}) collective-permute-start(bf16[1,128,1024]{2,1,0:T(8,128)(2,1)S(1)} %fusion.7), channel_id=1, source_target_pairs={{0,2},{1,3},{2,0},{3,1},{4,6},{5,7},{6,4},{7,5},{8,10},{9,11},{10,... | collective-permute-start | bytes 786440 | tf_op jit(solution)/shard_map/ppermute | solution.py:76
  123.2 6.4 %collective-permute-start.27 = (bf16[1,1,128,1024]{3,2,1,0:T(8,128)(2,1)S(1)}, bf16[1,1,128,1024]{3,2,1,0:T(8,128)(2,1)S(1)}, u32[]{:S(2)}, u32[]{:S(2)}) collective-permute-start(bf16[1,1,128,1024]{3,2,1,0:T(8,128)(2,1)S(1)} %fusion.9), channel_id=1, source_target_pairs={{0,16},{8,24},{16,0},{24,8},{1,17},{9,25},{17,1},{25,9},{2,18},{10... | collective-permute-start | bytes 786440 | tf_op jit(solution)/shard_map/ppermute | solution.py:76
  127.3 9.3 %collective-permute-start.18 = (bf16[128,1024]{1,0:T(8,128)(2,1)S(1)}, bf16[128,1024]{1,0:T(8,128)(2,1)S(1)}, u32[]{:S(2)}, u32[]{:S(2)}) collective-permute-start(bf16[128,1024]{1,0:T(8,128)(2,1)S(1)} %fusion.6.refs_5_), channel_id=1, source_target_pairs={{0,1},{2,0},{4,2},{6,4},{7,6},{5,7},{3,5},{1,3},{8,9},{10,8},{12,1... | collective-permute-start | bytes 786440 | tf_op jit(solution)/shard_map/ppermute | solution.py:59
  128.9 9.2 %collective-permute-start.17 = (bf16[128,1024]{1,0:T(8,128)(2,1)S(1)}, bf16[128,1024]{1,0:T(8,128)(2,1)S(1)}, u32[]{:S(2)}, u32[]{:S(2)}) collective-permute-start(bf16[128,1024]{1,0:T(8,128)(2,1)S(1)} %fusion.6.refs_5_), channel_id=1, source_target_pairs={{0,2},{2,4},{4,6},{6,7},{7,5},{5,3},{3,1},{1,0},{8,10},{10,12},{12... | collective-permute-start | bytes 786440 | tf_op jit(solution)/shard_map/ppermute | solution.py:58
  129.7 12.5 %collective-permute-start.29 = (bf16[128,1024]{1,0:T(8,128)(2,1)S(1)}, bf16[128,1024]{1,0:T(8,128)(2,1)S(1)}, u32[]{:S(2)}, u32[]{:S(2)}) collective-permute-start(bf16[128,1024]{1,0:T(8,128)(2,1)S(1)} %fusion.8.refs_14_), channel_id=1, source_target_pairs={{0,1},{2,0},{4,2},{6,4},{7,6},{5,7},{3,5},{1,3},{8,9},{10,8},{12,1... | collective-permute-start | bytes 786440 | tf_op jit(solution)/shard_map/ppermute | solution.py:59
  131.2 12.5 %collective-permute-start.28 = (bf16[128,1024]{1,0:T(8,128)(2,1)S(1)}, bf16[128,1024]{1,0:T(8,128)(2,1)S(1)}, u32[]{:S(2)}, u32[]{:S(2)}) collective-permute-start(bf16[128,1024]{1,0:T(8,128)(2,1)S(1)} %fusion.8.refs_14_), channel_id=1, source_target_pairs={{0,2},{2,4},{4,6},{6,7},{7,5},{5,3},{3,1},{1,0},{8,10},{10,12},{12... | collective-permute-start | bytes 786440 | tf_op jit(solution)/shard_map/ppermute | solution.py:58
  136.6 11.2 %collective-permute-start.20 = (bf16[128,1024]{1,0:T(8,128)(2,1)S(1)}, bf16[128,1024]{1,0:T(8,128)(2,1)S(1)}, u32[]{:S(2)}, u32[]{:S(2)}) collective-permute-start(bf16[128,1024]{1,0:T(8,128)(2,1)S(1)} %collective-permute-done.18.refs_7_), channel_id=1, source_target_pairs={{0,1},{2,0},{4,2},{6,4},{7,6},{5,7},{3,5},{1,3},{8,9},{10,8},{12,1... | collective-permute-start | bytes 786440 | tf_op jit(solution)/shard_map/ppermute | solution.py:59
  138.1 11.2 %collective-permute-start.19 = (bf16[128,1024]{1,0:T(8,128)(2,1)S(1)}, bf16[128,1024]{1,0:T(8,128)(2,1)S(1)}, u32[]{:S(2)}, u32[]{:S(2)}) collective-permute-start(bf16[128,1024]{1,0:T(8,128)(2,1)S(1)} %collective-permute-done.17.refs_6_), channel_id=1, source_target_pairs={{0,2},{2,4},{4,6},{6,7},{7,5},{5,3},{3,1},{1,0},{8,10},{10,12},{12... | collective-permute-start | bytes 786440 | tf_op jit(solution)/shard_map/ppermute | solution.py:58
  142.3 11.2 %collective-permute-start.31 = (bf16[128,1024]{1,0:T(8,128)(2,1)S(1)}, bf16[128,1024]{1,0:T(8,128)(2,1)S(1)}, u32[]{:S(2)}, u32[]{:S(2)}) collective-permute-start(bf16[128,1024]{1,0:T(8,128)(2,1)S(1)} %collective-permute-done.29.refs_16_), channel_id=1, source_target_pairs={{0,1},{2,0},{4,2},{6,4},{7,6},{5,7},{3,5},{1,3},{8,9},{10,8},{12,1... | collective-permute-start | bytes 786440 | tf_op jit(solution)/shard_map/ppermute | solution.py:59
  143.7 11.2 %collective-permute-start.30 = (bf16[128,1024]{1,0:T(8,128)(2,1)S(1)}, bf16[128,1024]{1,0:T(8,128)(2,1)S(1)}, u32[]{:S(2)}, u32[]{:S(2)}) collective-permute-start(bf16[128,1024]{1,0:T(8,128)(2,1)S(1)} %collective-permute-done.28.refs_15_), channel_id=1, source_target_pairs={{0,2},{2,4},{4,6},{6,7},{7,5},{5,3},{3,1},{1,0},{8,10},{10,12},{12... | collective-permute-start | bytes 786440 | tf_op jit(solution)/shard_map/ppermute | solution.py:58
  147.9 11.2 %collective-permute-start.22 = (bf16[128,1024]{1,0:T(8,128)(2,1)S(1)}, bf16[128,1024]{1,0:T(8,128)(2,1)S(1)}, u32[]{:S(2)}, u32[]{:S(2)}) collective-permute-start(bf16[128,1024]{1,0:T(8,128)(2,1)S(1)} %collective-permute-done.20.refs_9_), channel_id=1, source_target_pairs={{0,1},{2,0},{4,2},{6,4},{7,6},{5,7},{3,5},{1,3},{8,9},{10,8},{12,1... | collective-permute-start | bytes 786440 | tf_op jit(solution)/shard_map/ppermute | solution.py:59
  149.4 11.3 %collective-permute-start.21 = (bf16[128,1024]{1,0:T(8,128)(2,1)S(1)}, bf16[128,1024]{1,0:T(8,128)(2,1)S(1)}, u32[]{:S(2)}, u32[]{:S(2)}) collective-permute-start(bf16[128,1024]{1,0:T(8,128)(2,1)S(1)} %collective-permute-done.19.refs_8_), channel_id=1, source_target_pairs={{0,2},{2,4},{4,6},{6,7},{7,5},{5,3},{3,1},{1,0},{8,10},{10,12},{12... | collective-permute-start | bytes 786440 | tf_op jit(solution)/shard_map/ppermute | solution.py:58
  153.5 11.2 %collective-permute-start.33 = (bf16[128,1024]{1,0:T(8,128)(2,1)S(1)}, bf16[128,1024]{1,0:T(8,128)(2,1)S(1)}, u32[]{:S(2)}, u32[]{:S(2)}) collective-permute-start(bf16[128,1024]{1,0:T(8,128)(2,1)S(1)} %collective-permute-done.31.refs_18_), channel_id=1, source_target_pairs={{0,1},{2,0},{4,2},{6,4},{7,6},{5,7},{3,5},{1,3},{8,9},{10,8},{12,1... | collective-permute-start | bytes 786440 | tf_op jit(solution)/shard_map/ppermute | solution.py:59
  155.0 11.3 %collective-permute-start.32 = (bf16[128,1024]{1,0:T(8,128)(2,1)S(1)}, bf16[128,1024]{1,0:T(8,128)(2,1)S(1)}, u32[]{:S(2)}, u32[]{:S(2)}) collective-permute-start(bf16[128,1024]{1,0:T(8,128)(2,1)S(1)} %collective-permute-done.30.refs_17_), channel_id=1, source_target_pairs={{0,2},{2,4},{4,6},{6,7},{7,5},{5,3},{3,1},{1,0},{8,10},{10,12},{12... | collective-permute-start | bytes 786440 | tf_op jit(solution)/shard_map/ppermute | solution.py:58
  159.1 8.0 %collective-permute-start.24 = (bf16[64,1024]{1,0:T(8,128)(2,1)S(1)}, bf16[64,1024]{1,0:T(8,128)(2,1)S(1)}, u32[]{:S(2)}, u32[]{:S(2)}) collective-permute-start(bf16[64,1024]{1,0:T(8,128)(2,1)S(1)} %slice.166), channel_id=1, source_target_pairs={{0,1},{2,0},{4,2},{6,4},{7,6},{5,7},{3,5},{1,3},{8,9},{10,8},{12,1... | collective-permute-start | bytes 393224 | tf_op jit(solution)/shard_map/ppermute | solution.py:63
  160.7 7.3 %collective-permute-start.23 = (bf16[64,1024]{1,0:T(8,128)(2,1)S(1)}, bf16[64,1024]{1,0:T(8,128)(2,1)S(1)}, u32[]{:S(2)}, u32[]{:S(2)}) collective-permute-start(bf16[64,1024]{1,0:T(8,128)(2,1)S(1)} %slice.165), channel_id=1, source_target_pairs={{0,2},{2,4},{4,6},{6,7},{7,5},{5,3},{3,1},{1,0},{8,10},{10,12},{12... | collective-permute-start | bytes 393224 | tf_op jit(solution)/shard_map/ppermute | solution.py:62
  184.8 21.4 %collective-permute-start.36 = (bf16[4096,128]{1,0:T(8,128)(2,1)}, bf16[4096,128]{1,0:T(8,128)(2,1)}, u32[]{:S(2)}, u32[]{:S(2)}) collective-permute-start(bf16[4096,128]{1,0:T(8,128)(2,1)} %get-tuple-element.52), channel_id=1, source_target_pairs={{0,16},{8,24},{16,0},{24,8},{1,17},{9,25},{17,1},{25,9},{2,18},{10... | collective-permute-start | bytes 3145736 | tf_op jit(solution)/shard_map/ppermute | solution.py:76
  186.3 26.5 %all-to-all-start.1 = ((bf16[8,4,2,64,128]{4,3,2,1,0:T(8,128)(2,1)}), bf16[8,4,2,64,128]{4,3,2,1,0:T(8,128)(2,1)S(1)}, u32[]{:S(2)}, u32[]{:S(2)}) async-start(bf16[8,4,2,64,128]{4,3,2,1,0:T(8,128)(2,1)} %get-tuple-element.51), calls=%async_computation.1 | async-start | bytes 2097152 | tf_op jit(solution)/shard_map/all_to_all | solution.py:471
  (49 other events, 622.5 us)
